TPU v7x, 32 devices: a whole 2x2x4 slice. The times are simulated.
32 devices in a mesh: space: 16 (over z, y, x), orb: 2 (over core).
Axes of the slice: x: 2, y: 2, z: 4, core: 2. Of those that a mesh axis runs over, the one named last changes fastest.
Arguments:
- coefficients: float32 [2, 16, 128, 512], P(None, 'space', None, 'orb'), may hold values from -6 to 6
- margin: float32 [16, 16, 128, 128], P('space'), may hold values from -0.125 to 0.125
- step_matrix: float32 [16, 16, 128, 128], P('space'), may hold values from -0.1875 to 0.1875
- neighbours: int32 [16, 16], P('space'), may hold values from 0 to 15, as said below
- pattern: int32 [16, 16], P('space'), may hold values 0 or 1
Outputs:
- propagated: float32 [2, 16, 128, 512], P(None, 'space', None, 'orb')
- projections: float32 [2, 512, 512], P(None, 'space', 'orb')
Inputs may be any that keep to these rules, and one draw needn't show every extreme that they name: neighbours[i, 0] = i; every other entry is an atom block of a spatial domain at most 2 domains away from that of block i (domain = block index); the block of slot 1 lies 2 domains ahead of block i and the block of slot 2 lies 2 domains behind it, each clipped to the first and last domain.
All inputs are finite; a program needn't handle non-finite values. No bound on the sum of `pattern` on one device may be relied on, other than what follows from the above.
Results may differ from a plain program's by a relative error of at most 0.0001.
Values sent between devices are 32-bit elements; how exact they have to be, the bound alone decides.
A program may use at most 64 MiB of HBM per device.

v0:
```python
import jax
import jax.numpy as jnp
from jax import lax
from jax.sharding import PartitionSpec as P

REACH_DEV = 2
ORDER = 4


def shifted(value, axis, by):
    length = lax.axis_size(axis)
    pairs = [(i, i + by) for i in range(length) if 0 <= i + by < length]
    return lax.ppermute(value, axis, pairs)


def local(coefficients, margin, step_matrix, neighbours, pattern):
    blocks_here = coefficients.shape[1]
    block_width = coefficients.shape[2]
    columns = coefficients.shape[3]
    position = lax.axis_index("space")
    column_ids = jnp.arange(neighbours.shape[1], dtype=jnp.int32)[None, :]
    weights = jnp.where(column_ids == 0, jnp.float32(1.0), pattern.astype(jnp.float32))
    margin_live = margin * weights[:, :, None, None]
    step_live = step_matrix * weights[:, :, None, None]
    local_index = (neighbours - (position - REACH_DEV) * blocks_here).reshape(-1)

    def window_of(state):
        ahead = [shifted(state, "space", -distance) for distance in range(1, REACH_DEV + 1)]
        behind = [shifted(state, "space", distance) for distance in range(1, REACH_DEV + 1)]
        return jnp.concatenate(behind[::-1] + [state] + ahead, axis=0)

    def apply_blocks(matrix, state):
        window = window_of(state)
        picked = jnp.take(window, local_index, axis=0)
        picked = picked.reshape(blocks_here, -1, block_width, state.shape[2])
        return jnp.einsum("rkab,rkbc->rac", matrix, picked, precision=lax.Precision.HIGHEST)

    state = jnp.concatenate([coefficients[0], coefficients[1]], axis=-1)
    moved = state + apply_blocks(margin_live, state)
    total = moved
    term = moved
    for order_index in range(1, ORDER + 1):
        image = apply_blocks(step_live, term)
        term = jnp.concatenate([image[..., columns:], -image[..., :columns]], axis=-1) / order_index
        total = total + term
    propagated = jnp.stack([total[..., :columns], total[..., columns:]])
    reference_all = lax.all_gather(coefficients, "orb", axis=3, tiled=True)
    all_orbitals = reference_all.shape[3]
    old_real = reference_all[0].reshape(-1, all_orbitals)
    old_imag = reference_all[1].reshape(-1, all_orbitals)
    new_real = propagated[0].reshape(-1, columns)
    new_imag = propagated[1].reshape(-1, columns)
    highest = lax.Precision.HIGHEST
    part_real = jnp.einsum("ra,rb->ab", old_real, new_real, precision=highest) + jnp.einsum(
        "ra,rb->ab", old_imag, new_imag, precision=highest
    )
    part_imag = jnp.einsum("ra,rb->ab", old_real, new_imag, precision=highest) - jnp.einsum(
        "ra,rb->ab", old_imag, new_real, precision=highest
    )
    partial_value = jnp.stack([part_real, part_imag])
    rows_total = blocks_here * block_width * lax.axis_size("space")
    summed = lax.psum(partial_value, "space")
    share = all_orbitals // lax.axis_size("space")
    owned = lax.dynamic_slice_in_dim(summed, position * share, share, 1)
    return (propagated, owned / rows_total)


def solution(mesh):
    return jax.shard_map(
        local,
        mesh=mesh,
        in_specs=(
            P(None, "space", None, "orb"),
            P("space", None, None, None),
            P("space", None, None, None),
            P("space", None),
            P("space", None),
        ),
        out_specs=(P(None, "space", None, "orb"), P(None, "space", "orb")),
        check_vma=False,
    )
```

profile of v0, /device:TPU:0, one launch (start us, length us, event | category | flops | bytes accessed | tf_op | source)
XLA Modules:
  0.0 289.2 jit_solution(422266836856999475)
XLA Ops:
  7.2 0.0 all-reduce.2.cloned.1.call-start
  7.2 1.0 slice_bitcast_fusion.10
  8.3 4.9 %collective-permute-start = (f32[1,128,512]{2,1,0:T(8,128)S(1)}, f32[1,128,512]{2,1,0:T(8,128)S(1)}, u32[]{:S(2)}, u32[]{:S(2)}) collective-permute-start(f32[1,128,512]{2,1,0:T(8,128)S(1)} %pad_maximum_fusion.1), channel_id=1, source_target_pairs={{0,4},{2,6},{4,8},{6,10},{8,12},{10,14},{12,16},{14,18},{16,20},{1... | collective-permute-start | bytes 786440 | tf_op jit(solution)/shard_map/ppermute | solution.py:13
  13.2 3.4 %collective-permute-start.1 = (f32[1,128,512]{2,1,0:T(8,128)S(1)}, f32[1,128,512]{2,1,0:T(8,128)S(1)}, u32[]{:S(2)}, u32[]{:S(2)}) collective-permute-start(f32[1,128,512]{2,1,0:T(8,128)S(1)} %pad_maximum_fusion.1), channel_id=1, source_target_pairs={{0,2},{2,4},{4,6},{6,8},{8,10},{10,12},{12,14},{14,16},{16,18},{18... | collective-permute-start | bytes 786440 | tf_op jit(solution)/shard_map/ppermute | solution.py:13
  16.6 1.3 collective-permute-start.2
  17.9 1.3 collective-permute-start.3
  19.3 5.0 %collective-permute-done = f32[1,128,512]{2,1,0:T(8,128)S(1)} collective-permute-done((f32[1,128,512]{2,1,0:T(8,128)S(1)}, f32[1,128,512]{2,1,0:T(8,128)S(1)}, u32[]{:S(2)}, u32[]{:S(2)}) %collective-permute-start) | collective-permute-done | bytes 262176 | tf_op jit(solution)/shard_map/ppermute | solution.py:13
  24.3 0.2 collective-permute-done.1
  24.5 4.9 %collective-permute-done.2 = f32[1,128,512]{2,1,0:T(8,128)S(1)} collective-permute-done((f32[1,128,512]{2,1,0:T(8,128)S(1)}, f32[1,128,512]{2,1,0:T(8,128)S(1)}, u32[]{:S(2)}, u32[]{:S(2)}) %collective-permute-start.2) | collective-permute-done | bytes 262176 | tf_op jit(solution)/shard_map/ppermute | solution.py:13
  29.5 0.0 collective-permute-done.3
  29.5 0.0 copy-start.2
  29.5 2.8 gather_fusion
  32.3 4.2 %fusion.37 = f32[128,512]{1,0:T(8,128)S(1)} fusion(f32[16,128,512]{2,1,0:T(8,128)} %gather_fusion, pred[16]{0:T(512)(128)(4,1)S(1)} %get-tuple-element.5, f32[1,16,128,128]{3,2,1,0:T(8,128)S(1)} %copy-done.2, f32[16]{0:T(128)S(1)} %fusion.70, f32[128,256]{1,0:T(8,128)S(1)} %get-tuple-element.26, f32[128,256]{1,0:T(8,128)S(1)} %get-tuple-element.23), kind=kOutput, calls=%fused_computation.34 | convolution fusion | flops 1612054528 | bytes 5767248 | tf_op jit(solution)/shard_map/rkab,rkbc->rac/dot_general | solution.py:36
  36.5 8.1 %collective-permute-start.4 = (f32[1,128,512]{2,1,0:T(8,128)S(1)}, f32[1,128,512]{2,1,0:T(8,128)S(1)}, u32[]{:S(2)}, u32[]{:S(2)}) collective-permute-start(f32[1,128,512]{2,1,0:T(8,128)S(1)} %bitcast.91), channel_id=1, source_target_pairs={{0,4},{2,6},{4,8},{6,10},{8,12},{10,14},{12,16},{14,18},{16,20},{1... | collective-permute-start | bytes 786440 | tf_op jit(solution)/shard_map/ppermute | solution.py:13
  44.7 2.7 collective-permute-start.5
  47.4 1.3 collective-permute-start.6
  48.7 1.3 collective-permute-start.7
  50.0 4.3 %collective-permute-done.4 = f32[1,128,512]{2,1,0:T(8,128)S(1)} collective-permute-done((f32[1,128,512]{2,1,0:T(8,128)S(1)}, f32[1,128,512]{2,1,0:T(8,128)S(1)}, u32[]{:S(2)}, u32[]{:S(2)}) %collective-permute-start.4) | collective-permute-done | bytes 262176 | tf_op jit(solution)/shard_map/ppermute | solution.py:13
  54.3 0.0 collective-permute-done.5
  54.3 5.4 %collective-permute-done.6 = f32[1,128,512]{2,1,0:T(8,128)S(1)} collective-permute-done((f32[1,128,512]{2,1,0:T(8,128)S(1)}, f32[1,128,512]{2,1,0:T(8,128)S(1)}, u32[]{:S(2)}, u32[]{:S(2)}) %collective-permute-start.6) | collective-permute-done | bytes 262176 | tf_op jit(solution)/shard_map/ppermute | solution.py:13
  59.8 0.0 copy-start
  59.9 2.8 gather_fusion.1
  62.6 4.3 %fusion.25 = f32[1,128,512]{2,1,0:T(8,128)S(1)} fusion(f32[16,128,512]{2,1,0:T(8,128)} %gather_fusion.1, pred[16]{0:T(512)(128)(4,1)S(1)} %get-tuple-element.5, f32[1,16,128,128]{3,2,1,0:T(8,128)S(1)} %copy-done, f32[16]{0:T(128)S(1)} %fusion.70), kind=kOutput, calls=%fused_computation.30 | convolution fusion | flops 1611923456 | bytes 5505104 | tf_op jit(solution)/shard_map/rkab,rkbc->rac/dot_general | solution.py:36
  67.0 7.1 %collective-permute-start.8 = (f32[1,128,512]{2,1,0:T(8,128)S(1)}, f32[1,128,512]{2,1,0:T(8,128)S(1)}, u32[]{:S(2)}, u32[]{:S(2)}) collective-permute-start(f32[1,128,512]{2,1,0:T(8,128)S(1)} %pad_maximum_fusion.2), channel_id=1, source_target_pairs={{0,4},{2,6},{4,8},{6,10},{8,12},{10,14},{12,16},{14,18},{16,20},{1... | collective-permute-start | bytes 786440 | tf_op jit(solution)/shard_map/ppermute | solution.py:13
  74.1 3.4 %collective-permute-start.9 = (f32[1,128,512]{2,1,0:T(8,128)S(1)}, f32[1,128,512]{2,1,0:T(8,128)S(1)}, u32[]{:S(2)}, u32[]{:S(2)}) collective-permute-start(f32[1,128,512]{2,1,0:T(8,128)S(1)} %pad_maximum_fusion.2), channel_id=1, source_target_pairs={{0,2},{2,4},{4,6},{6,8},{8,10},{10,12},{12,14},{14,16},{16,18},{18... | collective-permute-start | bytes 786440 | tf_op jit(solution)/shard_map/ppermute | solution.py:13
  77.5 1.3 collective-permute-start.10
  78.8 1.3 collective-permute-start.11
  80.1 2.2 collective-permute-done.8
  82.3 2.0 collective-permute-done.9
  84.4 5.4 %collective-permute-done.10 = f32[1,128,512]{2,1,0:T(8,128)S(1)} collective-permute-done((f32[1,128,512]{2,1,0:T(8,128)S(1)}, f32[1,128,512]{2,1,0:T(8,128)S(1)}, u32[]{:S(2)}, u32[]{:S(2)}) %collective-permute-start.10) | collective-permute-done | bytes 262176 | tf_op jit(solution)/shard_map/ppermute | solution.py:13
  89.8 2.8 gather_fusion.2
  92.6 4.3 %fusion.28 = f32[1,128,512]{2,1,0:T(8,128)S(1)} fusion(f32[16,128,512]{2,1,0:T(8,128)} %gather_fusion.2, pred[16]{0:T(512)(128)(4,1)S(1)} %get-tuple-element.5, f32[1,16,128,128]{3,2,1,0:T(8,128)S(1)} %copy-done, f32[16]{0:T(128)S(1)} %fusion.70), kind=kOutput, calls=%fused_computation.31 | convolution fusion | flops 1611923456 | bytes 5505104 | tf_op jit(solution)/shard_map/rkab,rkbc->rac/dot_general | solution.py:36
  96.8 0.7 fusion.80
  97.6 6.7 %collective-permute-start.12 = (f32[1,128,512]{2,1,0:T(8,128)S(1)}, f32[1,128,512]{2,1,0:T(8,128)S(1)}, u32[]{:S(2)}, u32[]{:S(2)}) collective-permute-start(f32[1,128,512]{2,1,0:T(8,128)S(1)} %maximum_multiply_fusion.1), channel_id=1, source_target_pairs={{0,4},{2,6},{4,8},{6,10},{8,12},{10,14},{12,16},{14,18},{16,20},{1... | collective-permute-start | bytes 786440 | tf_op jit(solution)/shard_map/ppermute | solution.py:13
  104.3 2.9 %collective-permute-start.13 = (f32[1,128,512]{2,1,0:T(8,128)S(1)}, f32[1,128,512]{2,1,0:T(8,128)S(1)}, u32[]{:S(2)}, u32[]{:S(2)}) collective-permute-start(f32[1,128,512]{2,1,0:T(8,128)S(1)} %maximum_multiply_fusion.1), channel_id=1, source_target_pairs={{0,2},{2,4},{4,6},{6,8},{8,10},{10,12},{12,14},{14,16},{16,18},{18... | collective-permute-start | bytes 786440 | tf_op jit(solution)/shard_map/ppermute | solution.py:13
  107.2 1.3 collective-permute-start.14
  108.5 1.3 collective-permute-start.15
  109.8 2.7 collective-permute-done.12
  112.5 1.8 collective-permute-done.13
  114.3 5.7 %collective-permute-done.14 = f32[1,128,512]{2,1,0:T(8,128)S(1)} collective-permute-done((f32[1,128,512]{2,1,0:T(8,128)S(1)}, f32[1,128,512]{2,1,0:T(8,128)S(1)}, u32[]{:S(2)}, u32[]{:S(2)}) %collective-permute-start.14) | collective-permute-done | bytes 262176 | tf_op jit(solution)/shard_map/ppermute | solution.py:13
  120.1 2.8 gather_fusion.3
  122.9 4.3 %fusion.31 = f32[1,128,512]{2,1,0:T(8,128)S(1)} fusion(f32[16,128,512]{2,1,0:T(8,128)} %gather_fusion.3, pred[16]{0:T(512)(128)(4,1)S(1)} %get-tuple-element.5, f32[1,16,128,128]{3,2,1,0:T(8,128)S(1)} %copy-done, f32[16]{0:T(128)S(1)} %fusion.70), kind=kOutput, calls=%fused_computation.32 | convolution fusion | flops 1611923456 | bytes 5505104 | tf_op jit(solution)/shard_map/rkab,rkbc->rac/dot_general | solution.py:36
  127.1 0.0 copy-start.1
  127.2 0.7 fusion.79
  127.9 6.4 %collective-permute-start.16 = (f32[1,128,512]{2,1,0:T(8,128)S(1)}, f32[1,128,512]{2,1,0:T(8,128)S(1)}, u32[]{:S(2)}, u32[]{:S(2)}) collective-permute-start(f32[1,128,512]{2,1,0:T(8,128)S(1)} %maximum_multiply_fusion.3), channel_id=1, source_target_pairs={{0,4},{2,6},{4,8},{6,10},{8,12},{10,14},{12,16},{14,18},{16,20},{1... | collective-permute-start | bytes 786440 | tf_op jit(solution)/shard_map/ppermute | solution.py:13
  134.3 3.2 %collective-permute-start.17 = (f32[1,128,512]{2,1,0:T(8,128)S(1)}, f32[1,128,512]{2,1,0:T(8,128)S(1)}, u32[]{:S(2)}, u32[]{:S(2)}) collective-permute-start(f32[1,128,512]{2,1,0:T(8,128)S(1)} %maximum_multiply_fusion.3), channel_id=1, source_target_pairs={{0,2},{2,4},{4,6},{6,8},{8,10},{10,12},{12,14},{14,16},{16,18},{18... | collective-permute-start | bytes 786440 | tf_op jit(solution)/shard_map/ppermute | solution.py:13
  137.6 2.2 all_gather.3
  139.7 1.3 collective-permute-start.18
  141.0 1.5 collective-permute-start.19
  142.6 8.0 %collective-permute-done.18 = f32[1,128,512]{2,1,0:T(8,128)S(1)} collective-permute-done((f32[1,128,512]{2,1,0:T(8,128)S(1)}, f32[1,128,512]{2,1,0:T(8,128)S(1)}, u32[]{:S(2)}, u32[]{:S(2)}) %collective-permute-start.18) | collective-permute-done | bytes 262176 | tf_op jit(solution)/shard_map/ppermute | solution.py:13
  150.6 2.6 collective-permute-done.19
  153.2 2.8 gather_fusion.4
  156.0 4.3 %fusion.34 = f32[1,128,512]{2,1,0:T(8,128)S(1)} fusion(f32[16,128,512]{2,1,0:T(8,128)} %gather_fusion.4, pred[16]{0:T(512)(128)(4,1)S(1)} %get-tuple-element.5, f32[1,16,128,128]{3,2,1,0:T(8,128)S(1)} %copy-done, f32[16]{0:T(128)S(1)} %fusion.70), kind=kOutput, calls=%fused_computation.33 | convolution fusion | flops 1611923456 | bytes 5505104 | tf_op jit(solution)/shard_map/rkab,rkbc->rac/dot_general | solution.py:36
  160.4 0.1 fusion.58
  160.5 0.6 fusion.59
  161.1 0.6 fusion.60
  161.8 0.6 fusion.20
  162.4 0.6 fusion.21
  163.0 1.0 pad_maximum_fusion
  164.1 0.0 all-reduce.2.cloned.1.call-update
  164.1 0.7 pad_maximum_fusion.3
  164.8 115.7 %all-reduce.2.cloned.1.call-done = f32[2,512,256]{1,2,0:T(8,128)} async-done(((f32[2,512,256]{1,2,0:T(8,128)}), f32[2,512,256]{1,2,0:T(8,128)}) %all-reduce.2.cloned.1.call-update) | async-done | bytes 1048592 | tf_op jit(solution)/shard_map/psum | solution.py:62
  280.6 1.1 dynamic-slice_multiply_fusion
  281.7 0.7 copy.7
  (53 shorter events, 0.7 us)
Async XLA Ops:
  7.2 12.0 %copy-start.6 = (s32[1,16]{1,0:T(1,128)S(1)}, s32[1,16]{1,0:T(1,128)}, u32[]{:S(2)}) copy-start(s32[1,16]{1,0:T(1,128)} %param.10) | copy-start | bytes 196
  7.2 12.0 %copy-start.7 = (s32[1,16]{1,0:T(1,128)S(1)}, s32[1,16]{1,0:T(1,128)}, u32[]{:S(2)}) copy-start(s32[1,16]{1,0:T(1,128)} %param.11) | copy-start | bytes 196
  7.2 273.4 %all-reduce.2.cloned.1.call-start = ((), (), s32[]{:S(2)}) async-start(), calls=%async_computation | async-start | bytes 2097152 | tf_op jit(solution)/shard_map/psum | solution.py:62
  8.3 16.0 %collective-permute-start = (f32[1,128,512]{2,1,0:T(8,128)S(1)}, f32[1,128,512]{2,1,0:T(8,128)S(1)}, u32[]{:S(2)}, u32[]{:S(2)}) collective-permute-start(f32[1,128,512]{2,1,0:T(8,128)S(1)} %pad_maximum_fusion.1), channel_id=1, source_target_pairs={{0,4},{2,6},{4,8},{6,10},{8,12},{10,14},{12,16},{14,18},{16,20},{1... | collective-permute-start | bytes 786440 | tf_op jit(solution)/shard_map/ppermute | solution.py:13
  13.2 11.3 %collective-permute-start.1 = (f32[1,128,512]{2,1,0:T(8,128)S(1)}, f32[1,128,512]{2,1,0:T(8,128)S(1)}, u32[]{:S(2)}, u32[]{:S(2)}) collective-permute-start(f32[1,128,512]{2,1,0:T(8,128)S(1)} %pad_maximum_fusion.1), channel_id=1, source_target_pairs={{0,2},{2,4},{4,6},{6,8},{8,10},{10,12},{12,14},{14,16},{16,18},{18... | collective-permute-start | bytes 786440 | tf_op jit(solution)/shard_map/ppermute | solution.py:13
  16.6 12.9 %collective-permute-start.2 = (f32[1,128,512]{2,1,0:T(8,128)S(1)}, f32[1,128,512]{2,1,0:T(8,128)S(1)}, u32[]{:S(2)}, u32[]{:S(2)}) collective-permute-start(f32[1,128,512]{2,1,0:T(8,128)S(1)} %pad_maximum_fusion.1), channel_id=1, source_target_pairs={{2,0},{4,2},{6,4},{8,6},{10,8},{12,10},{14,12},{16,14},{18,16},{20... | collective-permute-start | bytes 786440 | tf_op jit(solution)/shard_map/ppermute | solution.py:13
  17.9 11.6 %collective-permute-start.3 = (f32[1,128,512]{2,1,0:T(8,128)S(1)}, f32[1,128,512]{2,1,0:T(8,128)S(1)}, u32[]{:S(2)}, u32[]{:S(2)}) collective-permute-start(f32[1,128,512]{2,1,0:T(8,128)S(1)} %pad_maximum_fusion.1), channel_id=1, source_target_pairs={{4,0},{6,2},{8,4},{10,6},{12,8},{14,10},{16,12},{18,14},{20,16},{2... | collective-permute-start | bytes 786440 | tf_op jit(solution)/shard_map/ppermute | solution.py:13
  29.5 2.8 copy-start.2
  36.5 17.7 %collective-permute-start.4 = (f32[1,128,512]{2,1,0:T(8,128)S(1)}, f32[1,128,512]{2,1,0:T(8,128)S(1)}, u32[]{:S(2)}, u32[]{:S(2)}) collective-permute-start(f32[1,128,512]{2,1,0:T(8,128)S(1)} %bitcast.91), channel_id=1, source_target_pairs={{0,4},{2,6},{4,8},{6,10},{8,12},{10,14},{12,16},{14,18},{16,20},{1... | collective-permute-start | bytes 786440 | tf_op jit(solution)/shard_map/ppermute | solution.py:13
  44.7 9.6 %collective-permute-start.5 = (f32[1,128,512]{2,1,0:T(8,128)S(1)}, f32[1,128,512]{2,1,0:T(8,128)S(1)}, u32[]{:S(2)}, u32[]{:S(2)}) collective-permute-start(f32[1,128,512]{2,1,0:T(8,128)S(1)} %bitcast.92), channel_id=1, source_target_pairs={{0,2},{2,4},{4,6},{6,8},{8,10},{10,12},{12,14},{14,16},{16,18},{18... | collective-permute-start | bytes 786440 | tf_op jit(solution)/shard_map/ppermute | solution.py:13
  47.4 12.4 %collective-permute-start.6 = (f32[1,128,512]{2,1,0:T(8,128)S(1)}, f32[1,128,512]{2,1,0:T(8,128)S(1)}, u32[]{:S(2)}, u32[]{:S(2)}) collective-permute-start(f32[1,128,512]{2,1,0:T(8,128)S(1)} %bitcast.93), channel_id=1, source_target_pairs={{2,0},{4,2},{6,4},{8,6},{10,8},{12,10},{14,12},{16,14},{18,16},{20... | collective-permute-start | bytes 786440 | tf_op jit(solution)/shard_map/ppermute | solution.py:13
  48.7 11.1 %collective-permute-start.7 = (f32[1,128,512]{2,1,0:T(8,128)S(1)}, f32[1,128,512]{2,1,0:T(8,128)S(1)}, u32[]{:S(2)}, u32[]{:S(2)}) collective-permute-start(f32[1,128,512]{2,1,0:T(8,128)S(1)} %bitcast.94), channel_id=1, source_target_pairs={{4,0},{6,2},{8,4},{10,6},{12,8},{14,10},{16,12},{18,14},{20,16},{2... | collective-permute-start | bytes 786440 | tf_op jit(solution)/shard_map/ppermute | solution.py:13
  59.8 2.8 copy-start
  67.0 15.3 %collective-permute-start.8 = (f32[1,128,512]{2,1,0:T(8,128)S(1)}, f32[1,128,512]{2,1,0:T(8,128)S(1)}, u32[]{:S(2)}, u32[]{:S(2)}) collective-permute-start(f32[1,128,512]{2,1,0:T(8,128)S(1)} %pad_maximum_fusion.2), channel_id=1, source_target_pairs={{0,4},{2,6},{4,8},{6,10},{8,12},{10,14},{12,16},{14,18},{16,20},{1... | collective-permute-start | bytes 786440 | tf_op jit(solution)/shard_map/ppermute | solution.py:13
  74.1 10.2 %collective-permute-start.9 = (f32[1,128,512]{2,1,0:T(8,128)S(1)}, f32[1,128,512]{2,1,0:T(8,128)S(1)}, u32[]{:S(2)}, u32[]{:S(2)}) collective-permute-start(f32[1,128,512]{2,1,0:T(8,128)S(1)} %pad_maximum_fusion.2), channel_id=1, source_target_pairs={{0,2},{2,4},{4,6},{6,8},{8,10},{10,12},{12,14},{14,16},{16,18},{18... | collective-permute-start | bytes 786440 | tf_op jit(solution)/shard_map/ppermute | solution.py:13
  77.5 12.3 %collective-permute-start.10 = (f32[1,128,512]{2,1,0:T(8,128)S(1)}, f32[1,128,512]{2,1,0:T(8,128)S(1)}, u32[]{:S(2)}, u32[]{:S(2)}) collective-permute-start(f32[1,128,512]{2,1,0:T(8,128)S(1)} %pad_maximum_fusion.2), channel_id=1, source_target_pairs={{2,0},{4,2},{6,4},{8,6},{10,8},{12,10},{14,12},{16,14},{18,16},{20... | collective-permute-start | bytes 786440 | tf_op jit(solution)/shard_map/ppermute | solution.py:13
  78.8 11.0 %collective-permute-start.11 = (f32[1,128,512]{2,1,0:T(8,128)S(1)}, f32[1,128,512]{2,1,0:T(8,128)S(1)}, u32[]{:S(2)}, u32[]{:S(2)}) collective-permute-start(f32[1,128,512]{2,1,0:T(8,128)S(1)} %pad_maximum_fusion.2), channel_id=1, source_target_pairs={{4,0},{6,2},{8,4},{10,6},{12,8},{14,10},{16,12},{18,14},{20,16},{2... | collective-permute-start | bytes 786440 | tf_op jit(solution)/shard_map/ppermute | solution.py:13
  97.6 14.9 %collective-permute-start.12 = (f32[1,128,512]{2,1,0:T(8,128)S(1)}, f32[1,128,512]{2,1,0:T(8,128)S(1)}, u32[]{:S(2)}, u32[]{:S(2)}) collective-permute-start(f32[1,128,512]{2,1,0:T(8,128)S(1)} %maximum_multiply_fusion.1), channel_id=1, source_target_pairs={{0,4},{2,6},{4,8},{6,10},{8,12},{10,14},{12,16},{14,18},{16,20},{1... | collective-permute-start | bytes 786440 | tf_op jit(solution)/shard_map/ppermute | solution.py:13
  104.3 10.0 %collective-permute-start.13 = (f32[1,128,512]{2,1,0:T(8,128)S(1)}, f32[1,128,512]{2,1,0:T(8,128)S(1)}, u32[]{:S(2)}, u32[]{:S(2)}) collective-permute-start(f32[1,128,512]{2,1,0:T(8,128)S(1)} %maximum_multiply_fusion.1), channel_id=1, source_target_pairs={{0,2},{2,4},{4,6},{6,8},{8,10},{10,12},{12,14},{14,16},{16,18},{18... | collective-permute-start | bytes 786440 | tf_op jit(solution)/shard_map/ppermute | solution.py:13
  107.2 12.8 %collective-permute-start.14 = (f32[1,128,512]{2,1,0:T(8,128)S(1)}, f32[1,128,512]{2,1,0:T(8,128)S(1)}, u32[]{:S(2)}, u32[]{:S(2)}) collective-permute-start(f32[1,128,512]{2,1,0:T(8,128)S(1)} %maximum_multiply_fusion.1), channel_id=1, source_target_pairs={{2,0},{4,2},{6,4},{8,6},{10,8},{12,10},{14,12},{16,14},{18,16},{20... | collective-permute-start | bytes 786440 | tf_op jit(solution)/shard_map/ppermute | solution.py:13
  108.5 11.6 %collective-permute-start.15 = (f32[1,128,512]{2,1,0:T(8,128)S(1)}, f32[1,128,512]{2,1,0:T(8,128)S(1)}, u32[]{:S(2)}, u32[]{:S(2)}) collective-permute-start(f32[1,128,512]{2,1,0:T(8,128)S(1)} %maximum_multiply_fusion.1), channel_id=1, source_target_pairs={{4,0},{6,2},{8,4},{10,6},{12,8},{14,10},{16,12},{18,14},{20,16},{2... | collective-permute-start | bytes 786440 | tf_op jit(solution)/shard_map/ppermute | solution.py:13
  127.1 10.4 %copy-start.1 = (f32[2,1,128,256]{3,2,1,0:T(8,128)S(1)}, f32[2,1,128,256]{3,2,1,0:T(8,128)}, u32[]{:S(2)}) copy-start(f32[2,1,128,256]{3,2,1,0:T(8,128)} %param.7) | copy-start | bytes 786436
  127.9 14.6 %collective-permute-start.16 = (f32[1,128,512]{2,1,0:T(8,128)S(1)}, f32[1,128,512]{2,1,0:T(8,128)S(1)}, u32[]{:S(2)}, u32[]{:S(2)}) collective-permute-start(f32[1,128,512]{2,1,0:T(8,128)S(1)} %maximum_multiply_fusion.3), channel_id=1, source_target_pairs={{0,4},{2,6},{4,8},{6,10},{8,12},{10,14},{12,16},{14,18},{16,20},{1... | collective-permute-start | bytes 786440 | tf_op jit(solution)/shard_map/ppermute | solution.py:13
  134.3 8.3 %collective-permute-start.17 = (f32[1,128,512]{2,1,0:T(8,128)S(1)}, f32[1,128,512]{2,1,0:T(8,128)S(1)}, u32[]{:S(2)}, u32[]{:S(2)}) collective-permute-start(f32[1,128,512]{2,1,0:T(8,128)S(1)} %maximum_multiply_fusion.3), channel_id=1, source_target_pairs={{0,2},{2,4},{4,6},{6,8},{8,10},{10,12},{12,14},{14,16},{16,18},{18... | collective-permute-start | bytes 786440 | tf_op jit(solution)/shard_map/ppermute | solution.py:13
  139.7 10.9 %collective-permute-start.18 = (f32[1,128,512]{2,1,0:T(8,128)S(1)}, f32[1,128,512]{2,1,0:T(8,128)S(1)}, u32[]{:S(2)}, u32[]{:S(2)}) collective-permute-start(f32[1,128,512]{2,1,0:T(8,128)S(1)} %maximum_multiply_fusion.3), channel_id=1, source_target_pairs={{2,0},{4,2},{6,4},{8,6},{10,8},{12,10},{14,12},{16,14},{18,16},{20... | collective-permute-start | bytes 786440 | tf_op jit(solution)/shard_map/ppermute | solution.py:13
  141.0 12.2 %collective-permute-start.19 = (f32[1,128,512]{2,1,0:T(8,128)S(1)}, f32[1,128,512]{2,1,0:T(8,128)S(1)}, u32[]{:S(2)}, u32[]{:S(2)}) collective-permute-start(f32[1,128,512]{2,1,0:T(8,128)S(1)} %maximum_multiply_fusion.3), channel_id=1, source_target_pairs={{4,0},{6,2},{8,4},{10,6},{12,8},{14,10},{16,12},{18,14},{20,16},{2... | collective-permute-start | bytes 786440 | tf_op jit(solution)/shard_map/ppermute | solution.py:13
  156.0 4.4 %copy-start.3 = (f32[128,256]{1,0:T(8,128)S(1)}, f32[128,256]{1,0:T(8,128)}, u32[]{:S(2)}) copy-start(f32[128,256]{1,0:T(8,128)} %get-tuple-element.17) | copy-start | bytes 393220
  156.0 4.4 %copy-start.4 = (f32[128,256]{1,0:T(8,128)S(1)}, f32[128,256]{1,0:T(8,128)}, u32[]{:S(2)}) copy-start(f32[128,256]{1,0:T(8,128)} %get-tuple-element.12) | copy-start | bytes 393220
  156.0 4.4 %copy-start.5 = (f32[128,256]{1,0:T(8,128)S(1)}, f32[128,256]{1,0:T(8,128)}, u32[]{:S(2)}) copy-start(f32[128,256]{1,0:T(8,128)} %get-tuple-element.13) | copy-start | bytes 393220
Sparse Core Ops, SparseCore 0:
  164.2 116.3 all-reduce.1
where the time goes:
time: 290 us; the launch traced here: 289 us
  waiting for transfers between devices  166 us (57%)
  starting transfers between devices  61.9 us (21%)
  matrix products  23.8 us (8%)
  local copies, waits for them, and re-layouts  16.1 us (6%)
  between operations  14.7 us (5%)
  other arithmetic  4.6 us (2%)
    psum x1, waiting for transfers between devices, local(): summed = lax.psum(partial_value, 'space')  116 us
    ppermute x20, starting transfers between devices, shifted(): return lax.ppermute(value, axis, pairs)  61.9 us
    ppermute x20, waiting for transfers between devices, shifted(): return lax.ppermute(value, axis, pairs)  50.2 us
    dot_general x5, matrix products, apply_blocks(): jnp.einsum('rkab,rkbc->rac', matrix, picked, precision=lax.Precision.HIGH...  21.3 us
    gather x5, local copies, waits for them, and re-layouts, apply_blocks(): picked = jnp.take(window, local_index, axis=0)  13.9 us
  transfers between devices with their start and end apart: 21, of which 14 were waited for; matrix products, arithmetic and copies ran while one was open for 0% of the time, Pallas kernels for 0%

commit v1 on v0

v1 whole, which is shorter than its diff:
```python
import functools

import jax
import jax.numpy as jnp
from jax import lax
from jax.experimental import pallas as pl
from jax.experimental.pallas import tpu as pltpu
from jax.sharding import PartitionSpec as P

REACH = 2
WIN = 2 * REACH + 1
ORDER = 4
GROUP = 4
BLOCK = 128
LANES = 128
HALF = BLOCK // 2
MESH = pl.DeviceIdType.MESH


def halves():
    lane = lax.broadcasted_iota(jnp.int32, (1, LANES), 1)
    return lane < LANES // 2


def swap(value):
    return pltpu.roll(value, LANES // 2, 1)


def split(value):
    high = value.astype(jnp.bfloat16)
    low = (value - high.astype(jnp.float32)).astype(jnp.bfloat16)
    return high, low


def product(high, low, both):
    wide = jnp.dot(high, both, preferred_element_type=jnp.float32)
    narrow = jnp.dot(low, both[:, :LANES], preferred_element_type=jnp.float32)
    return wide[:, :LANES] + wide[:, LANES:] + narrow


def kernel(
    spaces, coef, margin, step, nbr, pat, prop, proj,
    old, win, rows, mat_hi, mat_lo, both, total, old_hi, old_lo, part, got, back,
    a2a_s, a2a_r, mat_s, mat_r, fwd_s, fwd_r, old_s, old_r, oldx_s, oldx_r,
    halo_s, halo_r, back_s, back_r, part_s, part_r,
):
    share = proj.shape[1]
    quads = spaces // GROUP
    s = lax.axis_index("space")
    o = lax.axis_index("orb")
    q = s // GROUP
    m = s % GROUP
    base = q * GROUP
    other = 1 - o
    left = halves()

    barrier = pltpu.get_barrier_semaphore()

    @pl.loop(1, spaces)
    def _(j):
        pl.semaphore_signal(barrier, inc=1, device_id=((s + j) % spaces, o), device_id_type=MESH)

    pl.semaphore_signal(barrier, inc=1, device_id=(s, other), device_id_type=MESH)

    for t in range(2):
        columns = slice(t * LANES, (t + 1) * LANES)
        real = coef[0, 0, :, columns]
        imag = coef[1, 0, :, columns]
        old[o, 2 * t, m] = jnp.where(left, real, swap(imag))
        old[o, 2 * t + 1, m] = jnp.where(left, swap(real), imag)

    def compact(which, source):
        sums = [None] * WIN
        for k in range(nbr.shape[1]):
            block = source[0, k, pl.ds(pl.multiple_of(o * HALF, HALF), HALF), :]
            live = jnp.float32(1.0) if k == 0 else pat[0, k].astype(jnp.float32)
            for d in range(WIN):
                here = (nbr[0, k] == s + (d - REACH)).astype(jnp.float32) * live
                value = here * block
                sums[d] = value if sums[d] is None else sums[d] + value
        for d in range(WIN):
            rows[which, m, o, :, d * BLOCK:(d + 1) * BLOCK] = sums[d]

    compact(0, margin)

    for n in range(ORDER + 1):
        @pl.when(q == 0)
        def _():
            win[n, 0:REACH] = jnp.zeros((REACH, BLOCK, LANES), jnp.float32)

        @pl.when(q == quads - 1)
        def _():
            win[n, REACH + GROUP:] = jnp.zeros((REACH, BLOCK, LANES), jnp.float32)

    pl.semaphore_wait(barrier, spaces)

    def remote(src, dst, send, recv, where):
        return pltpu.make_async_remote_copy(
            src_ref=src, dst_ref=dst, send_sem=send, recv_sem=recv, device_id=where, device_id_type=MESH
        )

    def peer(j):
        return (m + j) % GROUP

    def a2a(j):
        return remote(old.at[o, peer(j), m], old.at[o, peer(j), m], a2a_s.at[j], a2a_r.at[j], (base + peer(j), o))

    def mat_copy(which, j):
        return remote(
            rows.at[which, m, o], rows.at[which, m, o], mat_s.at[which, j], mat_r.at[which, j], (base + peer(j), o)
        )

    def mat_forward(which, j):
        block = (m + GROUP - j) % GROUP
        return remote(
            rows.at[which, block, o], rows.at[which, block, o], fwd_s.at[which, j], fwd_r.at[which, j], (s, other)
        )

    def old_copy(j, i):
        g = (m + j + i) % GROUP
        return remote(old.at[o, g, m], old.at[o, g, m], old_s.at[j, i], old_r.at[j, i], (base + peer(j), o))

    def old_cross():
        return remote(old.at[o], old.at[o], oldx_s, oldx_r, (s, other))

    def halo_up(n):
        src = old.at[o, m, GROUP - REACH:GROUP] if n == 0 else win.at[n, GROUP:GROUP + REACH]
        return remote(src, win.at[n, 0:REACH], halo_s.at[n, 0], halo_r.at[n, 0], (s + GROUP, o))

    def halo_down(n):
        src = old.at[o, m, 0:REACH] if n == 0 else win.at[n, REACH:2 * REACH]
        return remote(
            src, win.at[n, REACH + GROUP:2 * REACH + GROUP], halo_s.at[n, 1], halo_r.at[n, 1], (s - GROUP, o)
        )

    def send_halo(n):
        @pl.when(q < quads - 1)
        def _():
            halo_up(n).start()

        @pl.when(q > 0)
        def _():
            halo_down(n).start()

    def wait_halo(n):
        @pl.when(q > 0)
        def _():
            halo_up(n).wait_recv()

        @pl.when(q < quads - 1)
        def _():
            halo_down(n).wait_recv()

    def done_halo(n):
        @pl.when(q < quads - 1)
        def _():
            halo_up(n).wait_send()

        @pl.when(q > 0)
        def _():
            halo_down(n).wait_send()

    def put(block, value):
        high, low = split(value)
        both[block * BLOCK:(block + 1) * BLOCK, :LANES] = high
        both[block * BLOCK:(block + 1) * BLOCK, LANES:] = low

    for j in range(1, GROUP):
        a2a(j).start()
    for j in range(1, GROUP):
        mat_copy(0, j).start()
    mat_forward(0, 0).start()
    compact(1, step)
    for j in range(1, GROUP):
        mat_copy(1, j).start()
    mat_forward(1, 0).start()

    for j in range(1, GROUP):
        a2a(j).wait_recv()
    send_halo(0)
    for j in range(1, GROUP):
        for i in range(1, GROUP):
            old_copy(j, i).start()
    for b in range(GROUP):
        put(REACH + b, old[o, m, b])

    def receive_matrix(which):
        for j in range(1, GROUP):
            mat_copy(which, j).wait_recv()
            mat_forward(which, j).start()
        for j in range(GROUP):
            mat_forward(which, j).wait_recv()
        for b in range(GROUP):
            for h in range(2):
                high, low = split(rows[which, b, h])
                mat_hi[which, b, h * HALF:(h + 1) * HALF] = high
                mat_lo[which, b, h * HALF:(h + 1) * HALF] = low

    def piece(which, b, first, last):
        columns = slice((first - b) * BLOCK, (last - b) * BLOCK)
        return product(
            mat_hi[which, b, :, columns], mat_lo[which, b, :, columns], both[first * BLOCK:last * BLOCK]
        )

    def inner(which):
        return [
            piece(which, b, max(b, REACH), min(b + WIN, REACH + GROUP)) for b in range(GROUP)
        ]

    def outer(which, n, sums):
        wait_halo(n)
        for w in (*range(REACH), *range(REACH + GROUP, 2 * REACH + GROUP)):
            put(w, win[n, w])
        result = []
        for b in range(GROUP):
            value = sums[b]
            if b < REACH:
                value = value + piece(which, b, b, REACH)
            if b + WIN > REACH + GROUP:
                value = value + piece(which, b, REACH + GROUP, b + WIN)
            result.append(value)
        return result

    receive_matrix(0)
    image = outer(0, 0, inner(0))
    for b in range(GROUP):
        moved = old[o, m, b] + image[b]
        win[1, REACH + b] = moved
        total[b] = moved
    send_halo(1)
    for b in range(GROUP):
        put(REACH + b, win[1, REACH + b])
    receive_matrix(1)

    for n in range(1, ORDER + 1):
        sums = inner(1)
        if n == 2:
            for j in range(1, GROUP):
                for i in range(1, GROUP):
                    old_copy(j, i).wait_recv()
            old_cross().start()
        if n == ORDER:
            old_cross().wait_recv()
            for core in range(2):
                for g in range(GROUP):
                    flat = old[core, g].reshape(GROUP * BLOCK, LANES)
                    high, low = split(flat.T)
                    old_hi[core * GROUP + g] = high
                    old_lo[core * GROUP + g] = low
        image = outer(1, n, sums)
        scale = jnp.where(left, jnp.float32(1.0 / n), jnp.float32(-1.0 / n))
        terms = [swap(value) * scale for value in image]
        if n < ORDER:
            for b in range(GROUP):
                win[n + 1, REACH + b] = terms[b]
            send_halo(n + 1)
        for b in range(GROUP):
            value = total[b] + terms[b]
            total[b] = value
            put(REACH + b, terms[b] if n < ORDER else value)

    def back_copy(j):
        return remote(total.at[peer(j)], back.at[m], back_s.at[j], back_r.at[j], (base + peer(j), o))

    for j in range(1, GROUP):
        back_copy(j).start()
    back[m] = total[m]

    sign = jnp.where(left, jnp.float32(1.0), jnp.float32(-1.0))
    new = both[REACH * BLOCK:(REACH + GROUP) * BLOCK]
    per = HALF // share
    for g in range(2 * GROUP):
        value = product(old_hi[g], old_lo[g], new)
        value = value[:HALF] + swap(value[HALF:]) * sign
        for r in range(per):
            part[g * per + r] = value[r * share:(r + 1) * share]

    def part_copy(j):
        to = (s + j) % spaces
        return remote(part.at[to], got.at[s], part_s.at[j], part_r.at[j], (to, o))

    @pl.loop(1, spaces)
    def _(j):
        part_copy(j).start()

    got[s] = part[s]

    for j in range(1, GROUP):
        back_copy(j).wait_recv()
    for t in range(2):
        columns = slice(t * LANES, (t + 1) * LANES)
        first = back[2 * t]
        second = back[2 * t + 1]
        prop[0, 0, :, columns] = jnp.where(left, first, swap(second))
        prop[1, 0, :, columns] = jnp.where(left, swap(first), second)

    for j in range(1, GROUP):
        a2a(j).wait_send()
        for which in range(2):
            mat_copy(which, j).wait_send()
        for i in range(1, GROUP):
            old_copy(j, i).wait_send()
        back_copy(j).wait_send()
    for j in range(GROUP):
        for which in range(2):
            mat_forward(which, j).wait_send()
    old_cross().wait_send()
    for n in range(ORDER + 1):
        done_halo(n)

    @pl.loop(1, spaces)
    def _(j):
        part_copy(j).wait_recv()

    sums = []
    for g in range(GROUP):
        value = got[g]
        for r in range(1, quads):
            value = value + got[r * GROUP + g]
        sums.append(value * (1.0 / (spaces * BLOCK)))
    for t in range(2):
        columns = slice(t * LANES, (t + 1) * LANES)
        first, second = sums[2 * t], sums[2 * t + 1]
        proj[0, :, columns] = jnp.where(left, first, swap(second))
        proj[1, :, columns] = jnp.where(left, swap(first), second)

    @pl.loop(1, spaces)
    def _(j):
        part_copy(j).wait_send()


def solution(mesh):
    spaces = mesh.shape["space"]
    dma = pltpu.SemaphoreType.DMA
    f32, bf16 = jnp.float32, jnp.bfloat16

    def local(coefficients, margin, step_matrix, neighbours, pattern):
        share = 2 * coefficients.shape[3] // spaces
        vmem = pl.BlockSpec(memory_space=pltpu.VMEM)
        smem = pl.BlockSpec(memory_space=pltpu.SMEM)
        return pl.pallas_call(
            functools.partial(kernel, spaces),
            out_shape=(
                jax.ShapeDtypeStruct(coefficients.shape, f32),
                jax.ShapeDtypeStruct((2, share, coefficients.shape[3]), f32),
            ),
            in_specs=[vmem, vmem, vmem, smem, smem],
            out_specs=(vmem, vmem),
            scratch_shapes=[
                pltpu.VMEM((2, GROUP, GROUP, BLOCK, LANES), f32),
                pltpu.VMEM((ORDER + 1, 2 * REACH + GROUP, BLOCK, LANES), f32),
                pltpu.VMEM((2, GROUP, 2, HALF, WIN * BLOCK), f32),
                pltpu.VMEM((2, GROUP, BLOCK, WIN * BLOCK), bf16),
                pltpu.VMEM((2, GROUP, BLOCK, WIN * BLOCK), bf16),
                pltpu.VMEM(((2 * REACH + GROUP) * BLOCK, 2 * LANES), bf16),
                pltpu.VMEM((GROUP, BLOCK, LANES), f32),
                pltpu.VMEM((2 * GROUP, LANES, GROUP * BLOCK), bf16),
                pltpu.VMEM((2 * GROUP, LANES, GROUP * BLOCK), bf16),
                pltpu.VMEM((spaces, share, LANES), f32),
                pltpu.VMEM((spaces, share, LANES), f32),
                pltpu.VMEM((GROUP, BLOCK, LANES), f32),
                dma((GROUP,)), dma((GROUP,)),
                dma((2, GROUP)), dma((2, GROUP)),
                dma((2, GROUP)), dma((2, GROUP)),
                dma((GROUP, GROUP)), dma((GROUP, GROUP)),
                dma, dma,
                dma((ORDER + 1, 2)), dma((ORDER + 1, 2)),
                dma((GROUP,)), dma((GROUP,)),
                dma((spaces,)), dma((spaces,)),
            ],
            compiler_params=pltpu.CompilerParams(
                collective_id=0, has_side_effects=True, vmem_limit_bytes=40 * 1024 * 1024
            ),
            cost_estimate=pl.CostEstimate(flops=1200000000, bytes_accessed=3000000, transcendentals=0),
        )(coefficients, margin, step_matrix, neighbours, pattern)

    return jax.shard_map(
        local,
        mesh=mesh,
        in_specs=(
            P(None, "space", None, "orb"),
            P("space", None, None, None),
            P("space", None, None, None),
            P("space", None),
            P("space", None),
        ),
        out_specs=(P(None, "space", None, "orb"), P(None, "space", "orb")),
        check_vma=False,
    )
```

time: 290 us -> 60.7 us (0.21)
  waiting for transfers between devices: 166 us -> 0 us
  starting transfers between devices: 61.9 us -> 0 us
  Pallas kernels: 0 us -> 53.7 us
  matrix products: 23.8 us -> 0 us
  between operations: 14.7 us -> 0.65 us
  local copies, waits for them, and re-layouts: 16.1 us -> 6.04 us
  other arithmetic: 4.6 us -> 0 us
    psum x1 -> x0, waiting for transfers between devices: 116 us -> none  [local(): summed = lax.psum(partial_value, 'space')]
    ppermute x20 -> x0, starting transfers between devices: 61.9 us -> none  [shifted(): return lax.ppermute(value, axis, pairs)]
    pallas_call x0 -> x1, Pallas kernels: none -> 53.7 us  [local(): pl.pallas_call(functools.partial(kernel, spaces), out_shape=(jax.ShapeDty...]
    ppermute x20 -> x0, waiting for transfers between devices: 50.2 us -> none  [shifted(): return lax.ppermute(value, axis, pairs)]
    dot_general x9 -> x0, matrix products: 23.8 us -> none  [the longest x5 21.3 us: apply_blocks(): jnp.einsum('rkab,rkbc->rac', matrix, picked, precision=lax.Precision.HIGH...]
    gather x5 -> x0, local copies, waits for them, and re-layouts: 13.9 us -> none  [apply_blocks(): picked = jnp.take(window, local_index, axis=0)]
    unnamed x33 -> x12, local copies, waits for them, and re-layouts: 1.08 us -> 6.04 us
  transfers between devices with their start and end apart: 21 -> 0, of which waited for: 14 -> 0; matrix products, arithmetic and copies ran while one was open for 0% -> 0% of each run, Pallas kernels for 0% -> 0%
where the time goes in v1:
time: 60.7 us; the launch traced here: 60.4 us
  Pallas kernels  53.7 us (88%)
  local copies, waits for them, and re-layouts  6.04 us (10%)
  between operations  0.65 us (1%)
    pallas_call x1, Pallas kernels, local(): pl.pallas_call(functools.partial(kernel, spaces), out_shape=(jax.ShapeDty...  53.7 us
    unnamed x12, local copies, waits for them, and re-layouts  6.04 us

profile of v1, /device:TPU:0, one launch (start us, length us, event | category | flops | bytes accessed | tf_op | source)
XLA Modules:
  0.0 60.4 jit_solution(12368393601155263334)
XLA Ops:
  0.6 0.0 copy-start
  0.6 1.2 %copy-done = f32[1,16,128,128]{3,2,1,0:T(8,128)S(1)} copy-done((f32[1,16,128,128]{3,2,1,0:T(8,128)S(1)}, f32[1,16,128,128]{3,2,1,0:T(8,128)}, u32[]{:S(2)}) %copy-start) | copy-done | bytes 1048600
  1.9 0.0 copy-start.1
  1.9 1.2 %copy-done.1 = f32[1,16,128,128]{3,2,1,0:T(8,128)S(1)} copy-done((f32[1,16,128,128]{3,2,1,0:T(8,128)S(1)}, f32[1,16,128,128]{3,2,1,0:T(8,128)}, u32[]{:S(2)}) %copy-start.1) | copy-done | bytes 1048600
  3.1 0.0 copy-start.2
  3.1 0.9 %copy-done.2 = f32[2,1,128,256]{3,2,1,0:T(8,128)S(1)} copy-done((f32[2,1,128,256]{3,2,1,0:T(8,128)S(1)}, f32[2,1,128,256]{3,2,1,0:T(8,128)}, u32[]{:S(2)}) %copy-start.2) | copy-done | bytes 262168
  4.0 0.0 copy-start.3
  4.0 0.7 %copy-done.3 = s32[1,16]{1,0:T(1,128)S(1)} copy-done((s32[1,16]{1,0:T(1,128)S(1)}, s32[1,16]{1,0:T(1,128)}, u32[]{:S(2)}) %copy-start.3) | copy-done | bytes 88
  4.7 0.0 copy-start.4
  4.7 0.7 %copy-done.4 = s32[1,16]{1,0:T(1,128)S(1)} copy-done((s32[1,16]{1,0:T(1,128)S(1)}, s32[1,16]{1,0:T(1,128)}, u32[]{:S(2)}) %copy-start.4) | copy-done | bytes 88
  5.3 53.7 %shard_map.68 = (f32[2,1,128,256]{3,2,1,0:T(8,128)S(1)}, f32[2,32,256]{2,1,0:T(8,128)S(1)}) custom-call(f32[2,1,128,256]{3,2,1,0:T(8,128)S(1)} %copy-done.2, f32[1,16,128,128]{3,2,1,0:T(8,128)S(1)} %copy-done, f32[1,16,128,128]{3,2,1,0:T(8,128)S(1)} %copy-done.1, s32[1,16]{1,0:T(1,128)S(1)} %copy-done.3, s32[1,16]{1,0:T(1,128)S(1)} %copy-done.4), custom_call_target="tpu_custom_call" | custom-call | flops 1200000000 | bytes 3000000 | tf_op jit(solution)/shard_map/pallas_call | solution.py:341
  59.1 0.7 %copy.9 = f32[2,1,128,256]{3,2,1,0:T(8,128)} copy(f32[2,1,128,256]{3,2,1,0:T(8,128)S(1)} %get-tuple-element.4) | data formatting | bytes 524288
  59.8 0.6 %copy.10 = f32[2,32,256]{2,1,0:T(8,128)} copy(f32[2,32,256]{2,1,0:T(8,128)S(1)} %get-tuple-element.5) | data formatting | bytes 131072
Async XLA Ops:
  0.6 1.2 %copy-start = (f32[1,16,128,128]{3,2,1,0:T(8,128)S(1)}, f32[1,16,128,128]{3,2,1,0:T(8,128)}, u32[]{:S(2)}) copy-start(f32[1,16,128,128]{3,2,1,0:T(8,128)} %margin.1) | copy-start | bytes 3145732
  1.9 1.2 %copy-start.1 = (f32[1,16,128,128]{3,2,1,0:T(8,128)S(1)}, f32[1,16,128,128]{3,2,1,0:T(8,128)}, u32[]{:S(2)}) copy-start(f32[1,16,128,128]{3,2,1,0:T(8,128)} %step.1) | copy-start | bytes 3145732
  3.1 0.9 %copy-start.2 = (f32[2,1,128,256]{3,2,1,0:T(8,128)S(1)}, f32[2,1,128,256]{3,2,1,0:T(8,128)}, u32[]{:S(2)}) copy-start(f32[2,1,128,256]{3,2,1,0:T(8,128)} %coef.1) | copy-start | bytes 786436
  4.0 0.7 %copy-start.3 = (s32[1,16]{1,0:T(1,128)S(1)}, s32[1,16]{1,0:T(1,128)}, u32[]{:S(2)}) copy-start(s32[1,16]{1,0:T(1,128)} %nbr.1) | copy-start | bytes 196
  4.7 0.7 %copy-start.4 = (s32[1,16]{1,0:T(1,128)S(1)}, s32[1,16]{1,0:T(1,128)}, u32[]{:S(2)}) copy-start(s32[1,16]{1,0:T(1,128)} %pat.1) | copy-start | bytes 196

commit v2 on v1

--- a/solution.py
+++ b/solution.py
@@ -39,9 +39,9 @@
 
 
 def kernel(
-    spaces, coef, margin, step, nbr, pat, prop, proj,
-    old, win, rows, mat_hi, mat_lo, both, total, old_hi, old_lo, part, got, back,
-    a2a_s, a2a_r, mat_s, mat_r, fwd_s, fwd_r, old_s, old_r, oldx_s, oldx_r,
+    spaces, coef_in, margin_in, step_in, nbr_in, pat_in, prop, proj,
+    coef, raw, nbr, pat, load_sem, old, win, rows, mat_hi, mat_lo, both, total, old_hi, old_lo, part, got, back,
+    a2a_s, a2a_r, mat_s, mat_r, dia_s, dia_r, fwd_s, fwd_r, old_s, old_r, oldx_s, oldx_r,
     halo_s, halo_r, back_s, back_r, part_s, part_r,
 ):
     share = proj.shape[1]
@@ -53,6 +53,19 @@
     base = q * GROUP
     other = 1 - o
     left = halves()
+    beside = (m + 1 - 2 * (m % 2), (m + GROUP // 2) % GROUP)
+    blocks = (m, beside[0], beside[1], (beside[0] + GROUP // 2) % GROUP)
+    mine = pl.ds(pl.multiple_of(o * HALF, HALF), HALF)
+
+    loads = [
+        pltpu.make_async_copy(coef_in.at[:, 0], coef, load_sem.at[0]),
+        pltpu.make_async_copy(nbr_in, nbr, load_sem.at[1]),
+        pltpu.make_async_copy(pat_in, pat, load_sem.at[2]),
+        pltpu.make_async_copy(margin_in.at[0, :, mine], raw.at[0], load_sem.at[3]),
+        pltpu.make_async_copy(step_in.at[0, :, mine], raw.at[1], load_sem.at[4]),
+    ]
+    for load in loads:
+        load.start()
 
     barrier = pltpu.get_barrier_semaphore()
 
@@ -62,26 +75,26 @@
 
     pl.semaphore_signal(barrier, inc=1, device_id=(s, other), device_id_type=MESH)
 
+    loads[0].wait()
     for t in range(2):
         columns = slice(t * LANES, (t + 1) * LANES)
-        real = coef[0, 0, :, columns]
-        imag = coef[1, 0, :, columns]
+        real = coef[0, :, columns]
+        imag = coef[1, :, columns]
         old[o, 2 * t, m] = jnp.where(left, real, swap(imag))
         old[o, 2 * t + 1, m] = jnp.where(left, swap(real), imag)
 
-    def compact(which, source):
+    def compact(which):
         sums = [None] * WIN
         for k in range(nbr.shape[1]):
-            block = source[0, k, pl.ds(pl.multiple_of(o * HALF, HALF), HALF), :]
+            block = raw[which, k]
             live = jnp.float32(1.0) if k == 0 else pat[0, k].astype(jnp.float32)
             for d in range(WIN):
                 here = (nbr[0, k] == s + (d - REACH)).astype(jnp.float32) * live
                 value = here * block
                 sums[d] = value if sums[d] is None else sums[d] + value
         for d in range(WIN):
-            rows[which, m, o, :, d * BLOCK:(d + 1) * BLOCK] = sums[d]
-
-    compact(0, margin)
+            for p in range(2):
+                rows[which, m, o, p, :, d * BLOCK:(d + 1) * BLOCK] = sums[d][p * HALF // 2:(p + 1) * HALF // 2]
 
     for n in range(ORDER + 1):
         @pl.when(q == 0)
@@ -105,16 +118,17 @@
     def a2a(j):
         return remote(old.at[o, peer(j), m], old.at[o, peer(j), m], a2a_s.at[j], a2a_r.at[j], (base + peer(j), o))
 
-    def mat_copy(which, j):
-        return remote(
-            rows.at[which, m, o], rows.at[which, m, o], mat_s.at[which, j], mat_r.at[which, j], (base + peer(j), o)
-        )
-
-    def mat_forward(which, j):
-        block = (m + GROUP - j) % GROUP
-        return remote(
-            rows.at[which, block, o], rows.at[which, block, o], fwd_s.at[which, j], fwd_r.at[which, j], (s, other)
-        )
+    def mat_copy(which, axis, p):
+        src = rows.at[which, m, o, p]
+        return remote(src, src, mat_s.at[which, axis, p], mat_r.at[which, axis, p], (base + beside[axis], o))
+
+    def mat_relay(which, p):
+        src = rows.at[which, beside[p], o, p]
+        return remote(src, src, dia_s.at[which, p], dia_r.at[which, p], (base + beside[1 - p], o))
+
+    def mat_cross(which, i, p):
+        src = rows.at[which, blocks[i], o, p]
+        return remote(src, src, fwd_s.at[which, i, p], fwd_r.at[which, i, p], (s, other))
 
     def old_copy(j, i):
         g = (m + j + i) % GROUP
@@ -167,32 +181,49 @@
 
     for j in range(1, GROUP):
         a2a(j).start()
-    for j in range(1, GROUP):
-        mat_copy(0, j).start()
-    mat_forward(0, 0).start()
-    compact(1, step)
-    for j in range(1, GROUP):
-        mat_copy(1, j).start()
-    mat_forward(1, 0).start()
+    for load in loads[1:4]:
+        load.wait()
+
+    def send_matrix(which):
+        for p in range(2):
+            mat_copy(which, p, p).start()
+        for p in range(2):
+            mat_copy(which, 1 - p, p).start()
+        for p in range(2):
+            mat_cross(which, 0, p).start()
+
+    def relay_matrix(which):
+        for p in range(2):
+            mat_copy(which, p, p).wait_recv()
+            mat_relay(which, p).start()
+            mat_cross(which, 1 + p, p).start()
+
+    compact(0)
+    send_matrix(0)
+    loads[4].wait()
+    compact(1)
 
     for j in range(1, GROUP):
         a2a(j).wait_recv()
     send_halo(0)
-    for j in range(1, GROUP):
-        for i in range(1, GROUP):
-            old_copy(j, i).start()
     for b in range(GROUP):
         put(REACH + b, old[o, m, b])
+    relay_matrix(0)
+    send_matrix(1)
 
     def receive_matrix(which):
-        for j in range(1, GROUP):
-            mat_copy(which, j).wait_recv()
-            mat_forward(which, j).start()
-        for j in range(GROUP):
-            mat_forward(which, j).wait_recv()
+        for p in range(2):
+            mat_copy(which, 1 - p, p).wait_recv()
+            mat_cross(which, 2 - p, p).start()
+        for p in range(2):
+            mat_relay(which, p).wait_recv()
+            mat_cross(which, 3, p).start()
+        for i in range(GROUP):
+            for p in range(2):
+                mat_cross(which, i, p).wait_recv()
         for b in range(GROUP):
             for h in range(2):
-                high, low = split(rows[which, b, h])
+                high, low = split(rows[which, b, h].reshape(HALF, WIN * BLOCK))
                 mat_hi[which, b, h * HALF:(h + 1) * HALF] = high
                 mat_lo[which, b, h * HALF:(h + 1) * HALF] = low
 
@@ -230,23 +261,29 @@
     send_halo(1)
     for b in range(GROUP):
         put(REACH + b, win[1, REACH + b])
+    relay_matrix(1)
+    for j in range(1, GROUP):
+        for i in range(1, GROUP):
+            old_copy(j, i).start()
     receive_matrix(1)
+
+    def turn(core):
+        for g in range(GROUP):
+            high, low = split(old[core, g].reshape(GROUP * BLOCK, LANES).T)
+            old_hi[core * GROUP + g] = high
+            old_lo[core * GROUP + g] = low
 
     for n in range(1, ORDER + 1):
         sums = inner(1)
-        if n == 2:
+        if n == ORDER - 1:
             for j in range(1, GROUP):
                 for i in range(1, GROUP):
                     old_copy(j, i).wait_recv()
             old_cross().start()
+            turn(o)
         if n == ORDER:
             old_cross().wait_recv()
-            for core in range(2):
-                for g in range(GROUP):
-                    flat = old[core, g].reshape(GROUP * BLOCK, LANES)
-                    high, low = split(flat.T)
-                    old_hi[core * GROUP + g] = high
-                    old_lo[core * GROUP + g] = low
+            turn(other)
         image = outer(1, n, sums)
         scale = jnp.where(left, jnp.float32(1.0 / n), jnp.float32(-1.0 / n))
         terms = [swap(value) * scale for value in image]
@@ -269,19 +306,22 @@
     sign = jnp.where(left, jnp.float32(1.0), jnp.float32(-1.0))
     new = both[REACH * BLOCK:(REACH + GROUP) * BLOCK]
     per = HALF // share
-    for g in range(2 * GROUP):
+
+    def part_copy(j):
+        to = (s + j) % spaces
+        return remote(part.at[to], got.at[s], part_s.at[j], part_r.at[j], (to, o))
+
+    for i in range(2 * GROUP):
+        g = (i + (q + quads // 2) * 2 * GROUP // quads) % (2 * GROUP)
         value = product(old_hi[g], old_lo[g], new)
         value = value[:HALF] + swap(value[HALF:]) * sign
         for r in range(per):
-            part[g * per + r] = value[r * share:(r + 1) * share]
-
-    def part_copy(j):
-        to = (s + j) % spaces
-        return remote(part.at[to], got.at[s], part_s.at[j], part_r.at[j], (to, o))
-
-    @pl.loop(1, spaces)
-    def _(j):
-        part_copy(j).start()
+            to = g * per + r
+            part[to] = value[r * share:(r + 1) * share]
+
+            @pl.when(to != s)
+            def _():
+                part_copy((to - s + spaces) % spaces).start()
 
     got[s] = part[s]
 
@@ -296,14 +336,16 @@
 
     for j in range(1, GROUP):
         a2a(j).wait_send()
-        for which in range(2):
-            mat_copy(which, j).wait_send()
         for i in range(1, GROUP):
             old_copy(j, i).wait_send()
         back_copy(j).wait_send()
-    for j in range(GROUP):
-        for which in range(2):
-            mat_forward(which, j).wait_send()
+    for which in range(2):
+        for p in range(2):
+            mat_copy(which, 0, p).wait_send()
+            mat_copy(which, 1, p).wait_send()
+            mat_relay(which, p).wait_send()
+            for i in range(GROUP):
+                mat_cross(which, i, p).wait_send()
     old_cross().wait_send()
     for n in range(ORDER + 1):
         done_halo(n)
@@ -337,19 +379,24 @@
     def local(coefficients, margin, step_matrix, neighbours, pattern):
         share = 2 * coefficients.shape[3] // spaces
         vmem = pl.BlockSpec(memory_space=pltpu.VMEM)
-        smem = pl.BlockSpec(memory_space=pltpu.SMEM)
+        hbm = pl.BlockSpec(memory_space=pltpu.HBM)
         return pl.pallas_call(
             functools.partial(kernel, spaces),
             out_shape=(
                 jax.ShapeDtypeStruct(coefficients.shape, f32),
                 jax.ShapeDtypeStruct((2, share, coefficients.shape[3]), f32),
             ),
-            in_specs=[vmem, vmem, vmem, smem, smem],
+            in_specs=[hbm] * 5,
             out_specs=(vmem, vmem),
             scratch_shapes=[
+                pltpu.VMEM((2,) + coefficients.shape[2:], f32),
+                pltpu.VMEM((2, margin.shape[1], HALF, BLOCK), f32),
+                pltpu.SMEM(neighbours.shape, jnp.int32),
+                pltpu.SMEM(pattern.shape, jnp.int32),
+                dma((5,)),
                 pltpu.VMEM((2, GROUP, GROUP, BLOCK, LANES), f32),
                 pltpu.VMEM((ORDER + 1, 2 * REACH + GROUP, BLOCK, LANES), f32),
-                pltpu.VMEM((2, GROUP, 2, HALF, WIN * BLOCK), f32),
+                pltpu.VMEM((2, GROUP, 2, 2, HALF // 2, WIN * BLOCK), f32),
                 pltpu.VMEM((2, GROUP, BLOCK, WIN * BLOCK), bf16),
                 pltpu.VMEM((2, GROUP, BLOCK, WIN * BLOCK), bf16),
                 pltpu.VMEM(((2 * REACH + GROUP) * BLOCK, 2 * LANES), bf16),
@@ -360,8 +407,9 @@
                 pltpu.VMEM((spaces, share, LANES), f32),
                 pltpu.VMEM((GROUP, BLOCK, LANES), f32),
                 dma((GROUP,)), dma((GROUP,)),
-                dma((2, GROUP)), dma((2, GROUP)),
-                dma((2, GROUP)), dma((2, GROUP)),
+                dma((2, 2, 2)), dma((2, 2, 2)),
+                dma((2, 2)), dma((2, 2)),
+                dma((2, GROUP, 2)), dma((2, GROUP, 2)),
                 dma((GROUP, GROUP)), dma((GROUP, GROUP)),
                 dma, dma,
                 dma((ORDER + 1, 2)), dma((ORDER + 1, 2)),

time: 60.7 us -> 55 us (0.906)
  Pallas kernels: 53.7 us -> 48 us
    pallas_call x1, Pallas kernels: 53.7 us -> 48 us  [local(): pl.pallas_call(functools.partial(kernel, spaces), out_shape=(jax.ShapeDty...]
where the time goes in v2:
time: 55 us; the launch traced here: 54.7 us
  Pallas kernels  48 us (87%)
  local copies, waits for them, and re-layouts  6.04 us (11%)
  between operations  0.65 us (1%)
    pallas_call x1, Pallas kernels, local(): pl.pallas_call(functools.partial(kernel, spaces), out_shape=(jax.ShapeDty...  48 us
    unnamed x12, local copies, waits for them, and re-layouts  6.04 us

profile of v2, /device:TPU:0, one launch (start us, length us, event | category | flops | bytes accessed | tf_op | source)
XLA Modules:
  0.0 54.7 jit_solution(6651960313548805453)
XLA Ops:
  0.6 0.0 copy-start
  0.6 1.2 %copy-done = f32[1,16,128,128]{3,2,1,0:T(8,128)S(1)} copy-done((f32[1,16,128,128]{3,2,1,0:T(8,128)S(1)}, f32[1,16,128,128]{3,2,1,0:T(8,128)}, u32[]{:S(2)}) %copy-start) | copy-done | bytes 1048600
  1.9 0.0 copy-start.1
  1.9 1.2 %copy-done.1 = f32[1,16,128,128]{3,2,1,0:T(8,128)S(1)} copy-done((f32[1,16,128,128]{3,2,1,0:T(8,128)S(1)}, f32[1,16,128,128]{3,2,1,0:T(8,128)}, u32[]{:S(2)}) %copy-start.1) | copy-done | bytes 1048600
  3.1 0.0 copy-start.2
  3.1 0.9 %copy-done.2 = f32[2,1,128,256]{3,2,1,0:T(8,128)S(1)} copy-done((f32[2,1,128,256]{3,2,1,0:T(8,128)S(1)}, f32[2,1,128,256]{3,2,1,0:T(8,128)}, u32[]{:S(2)}) %copy-start.2) | copy-done | bytes 262168
  4.0 0.0 copy-start.3
  4.0 0.7 %copy-done.3 = s32[1,16]{1,0:T(1,128)S(1)} copy-done((s32[1,16]{1,0:T(1,128)S(1)}, s32[1,16]{1,0:T(1,128)}, u32[]{:S(2)}) %copy-start.3) | copy-done | bytes 88
  4.7 0.0 copy-start.4
  4.7 0.7 %copy-done.4 = s32[1,16]{1,0:T(1,128)S(1)} copy-done((s32[1,16]{1,0:T(1,128)S(1)}, s32[1,16]{1,0:T(1,128)}, u32[]{:S(2)}) %copy-start.4) | copy-done | bytes 88
  5.3 48.0 %shard_map.68 = (f32[2,1,128,256]{3,2,1,0:T(8,128)S(1)}, f32[2,32,256]{2,1,0:T(8,128)S(1)}) custom-call(f32[2,1,128,256]{3,2,1,0:T(8,128)S(1)} %copy-done.2, f32[1,16,128,128]{3,2,1,0:T(8,128)S(1)} %copy-done, f32[1,16,128,128]{3,2,1,0:T(8,128)S(1)} %copy-done.1, s32[1,16]{1,0:T(1,128)S(1)} %copy-done.3, s32[1,16]{1,0:T(1,128)S(1)} %copy-done.4), custom_call_target="tpu_custom_call" | custom-call | flops 1200000000 | bytes 3000000 | tf_op jit(solution)/shard_map/pallas_call | solution.py:383
  53.4 0.7 %copy.9 = f32[2,1,128,256]{3,2,1,0:T(8,128)} copy(f32[2,1,128,256]{3,2,1,0:T(8,128)S(1)} %get-tuple-element.4) | data formatting | bytes 524288
  54.1 0.6 %copy.10 = f32[2,32,256]{2,1,0:T(8,128)} copy(f32[2,32,256]{2,1,0:T(8,128)S(1)} %get-tuple-element.5) | data formatting | bytes 131072
Async XLA Ops:
  0.6 1.2 %copy-start = (f32[1,16,128,128]{3,2,1,0:T(8,128)S(1)}, f32[1,16,128,128]{3,2,1,0:T(8,128)}, u32[]{:S(2)}) copy-start(f32[1,16,128,128]{3,2,1,0:T(8,128)} %margin_in.1) | copy-start | bytes 3145732
  1.9 1.2 %copy-start.1 = (f32[1,16,128,128]{3,2,1,0:T(8,128)S(1)}, f32[1,16,128,128]{3,2,1,0:T(8,128)}, u32[]{:S(2)}) copy-start(f32[1,16,128,128]{3,2,1,0:T(8,128)} %step_in.1) | copy-start | bytes 3145732
  3.1 0.9 %copy-start.2 = (f32[2,1,128,256]{3,2,1,0:T(8,128)S(1)}, f32[2,1,128,256]{3,2,1,0:T(8,128)}, u32[]{:S(2)}) copy-start(f32[2,1,128,256]{3,2,1,0:T(8,128)} %coef_in.1) | copy-start | bytes 786436
  4.0 0.7 %copy-start.3 = (s32[1,16]{1,0:T(1,128)S(1)}, s32[1,16]{1,0:T(1,128)}, u32[]{:S(2)}) copy-start(s32[1,16]{1,0:T(1,128)} %nbr_in.1) | copy-start | bytes 196
  4.7 0.7 %copy-start.4 = (s32[1,16]{1,0:T(1,128)S(1)}, s32[1,16]{1,0:T(1,128)}, u32[]{:S(2)}) copy-start(s32[1,16]{1,0:T(1,128)} %pat_in.1) | copy-start | bytes 196

commit v3 on v2

--- a/solution.py
+++ b/solution.py
@@ -17,13 +17,28 @@
 MESH = pl.DeviceIdType.MESH
 
 
-def halves():
-    lane = lax.broadcasted_iota(jnp.int32, (1, LANES), 1)
-    return lane < LANES // 2
-
-
-def swap(value):
-    return pltpu.roll(value, LANES // 2, 1)
+CHUNKS = 2
+QUARTER = LANES // 4
+
+
+def lanes():
+    return lax.broadcasted_iota(jnp.int32, (1, LANES), 1)
+
+
+def pair(even, first, second):
+    ahead = jnp.where(even, first, pltpu.roll(second, QUARTER, 1))
+    behind = jnp.where(even, pltpu.roll(first, LANES - QUARTER, 1), second)
+    return ahead, behind
+
+
+def swap(even, value):
+    return jnp.where(even, pltpu.roll(value, LANES - QUARTER, 1), pltpu.roll(value, QUARTER, 1))
+
+
+def cross(left, first, second):
+    ahead = jnp.where(left, first, pltpu.roll(second, LANES // 2, 1))
+    behind = jnp.where(left, pltpu.roll(first, LANES // 2, 1), second)
+    return ahead, behind
 
 
 def split(value):
@@ -40,7 +55,7 @@
 
 def kernel(
     spaces, coef_in, margin_in, step_in, nbr_in, pat_in, prop, proj,
-    coef, raw, nbr, pat, load_sem, old, win, rows, mat_hi, mat_lo, both, total, old_hi, old_lo, part, got, back,
+    coef, raw, nbr, pat, load_sem, old, edge, halo, state, rows, mat, both, total, blocks_new, new, old_hi, old_lo, part, got, back,
     a2a_s, a2a_r, mat_s, mat_r, dia_s, dia_r, fwd_s, fwd_r, old_s, old_r, oldx_s, oldx_r,
     halo_s, halo_r, back_s, back_r, part_s, part_r,
 ):
@@ -52,7 +67,8 @@
     m = s % GROUP
     base = q * GROUP
     other = 1 - o
-    left = halves()
+    left = lanes() < LANES // 2
+    even = lanes() % (2 * QUARTER) < QUARTER
     beside = (m + 1 - 2 * (m % 2), (m + GROUP // 2) % GROUP)
     blocks = (m, beside[0], beside[1], (beside[0] + GROUP // 2) % GROUP)
     mine = pl.ds(pl.multiple_of(o * HALF, HALF), HALF)
@@ -80,8 +96,7 @@
         columns = slice(t * LANES, (t + 1) * LANES)
         real = coef[0, :, columns]
         imag = coef[1, :, columns]
-        old[o, 2 * t, m] = jnp.where(left, real, swap(imag))
-        old[o, 2 * t + 1, m] = jnp.where(left, swap(real), imag)
+        old[o, 2 * t, m], old[o, 2 * t + 1, m] = pair(even, real, imag)
 
     def compact(which):
         sums = [None] * WIN
@@ -96,14 +111,21 @@
             for p in range(2):
                 rows[which, m, o, p, :, d * BLOCK:(d + 1) * BLOCK] = sums[d][p * HALF // 2:(p + 1) * HALF // 2]
 
-    for n in range(ORDER + 1):
-        @pl.when(q == 0)
-        def _():
-            win[n, 0:REACH] = jnp.zeros((REACH, BLOCK, LANES), jnp.float32)
-
-        @pl.when(q == quads - 1)
-        def _():
-            win[n, REACH + GROUP:] = jnp.zeros((REACH, BLOCK, LANES), jnp.float32)
+    def clear(side):
+        zero = jnp.zeros((BLOCK, LANES), jnp.float32)
+        for w in range(REACH):
+            edge[side, w] = zero
+        for n in range(ORDER):
+            for c in range(CHUNKS):
+                halo[n, c, side] = zero
+
+    @pl.when(q == 0)
+    def _():
+        clear(0)
+
+    @pl.when(q == quads - 1)
+    def _():
+        clear(1)
 
     pl.semaphore_wait(barrier, spaces)
 
@@ -137,47 +159,56 @@
     def old_cross():
         return remote(old.at[o], old.at[o], oldx_s, oldx_r, (s, other))
 
-    def halo_up(n):
-        src = old.at[o, m, GROUP - REACH:GROUP] if n == 0 else win.at[n, GROUP:GROUP + REACH]
-        return remote(src, win.at[n, 0:REACH], halo_s.at[n, 0], halo_r.at[n, 0], (s + GROUP, o))
-
-    def halo_down(n):
-        src = old.at[o, m, 0:REACH] if n == 0 else win.at[n, REACH:2 * REACH]
-        return remote(
-            src, win.at[n, REACH + GROUP:2 * REACH + GROUP], halo_s.at[n, 1], halo_r.at[n, 1], (s - GROUP, o)
-        )
-
-    def send_halo(n):
+    def halo_copy(n, c, up):
+        side = 0 if up else 1
+        if n == 0:
+            src = old.at[o, m, REACH:GROUP] if up else old.at[o, m, 0:REACH]
+            dst = edge.at[side]
+        else:
+            src, dst = state.at[n - 1, c, 1 - side], halo.at[n - 1, c, side]
+        to = s + GROUP if up else s - GROUP
+        return remote(src, dst, halo_s.at[n, c, side], halo_r.at[n, c, side], (to, o))
+
+    def send_halo(n, c):
         @pl.when(q < quads - 1)
         def _():
-            halo_up(n).start()
+            halo_copy(n, c, True).start()
 
         @pl.when(q > 0)
         def _():
-            halo_down(n).start()
-
-    def wait_halo(n):
+            halo_copy(n, c, False).start()
+
+    def wait_halo(n, c):
         @pl.when(q > 0)
         def _():
-            halo_up(n).wait_recv()
+            halo_copy(n, c, True).wait_recv()
 
         @pl.when(q < quads - 1)
         def _():
-            halo_down(n).wait_recv()
-
-    def done_halo(n):
+            halo_copy(n, c, False).wait_recv()
+
+    def done_halo(n, c):
         @pl.when(q < quads - 1)
         def _():
-            halo_up(n).wait_send()
+            halo_copy(n, c, True).wait_send()
 
         @pl.when(q > 0)
         def _():
-            halo_down(n).wait_send()
-
-    def put(block, value):
-        high, low = split(value)
-        both[block * BLOCK:(block + 1) * BLOCK, :LANES] = high
-        both[block * BLOCK:(block + 1) * BLOCK, LANES:] = low
+            halo_copy(n, c, False).wait_send()
+
+    def halves(value):
+        high = value.astype(jnp.bfloat16).astype(jnp.float32)
+        ahead, behind = cross(left, high, value - high)
+        return ahead.astype(jnp.bfloat16), behind.astype(jnp.bfloat16)
+
+    def span(w):
+        return slice(w * BLOCK, (w + 1) * BLOCK)
+
+    def put_block(w, value):
+        both[0, span(w)], both[1, span(w)] = halves(value)
+
+    def put_pair(c, w, value):
+        both[c, span(w)], both[c, span(w + 1)] = halves(value)
 
     for j in range(1, GROUP):
         a2a(j).start()
@@ -205,9 +236,9 @@
 
     for j in range(1, GROUP):
         a2a(j).wait_recv()
-    send_halo(0)
+    send_halo(0, 0)
     for b in range(GROUP):
-        put(REACH + b, old[o, m, b])
+        put_block(REACH + b, old[o, m, b])
     relay_matrix(0)
     send_matrix(1)
 
@@ -224,43 +255,49 @@
         for b in range(GROUP):
             for h in range(2):
                 high, low = split(rows[which, b, h].reshape(HALF, WIN * BLOCK))
-                mat_hi[which, b, h * HALF:(h + 1) * HALF] = high
-                mat_lo[which, b, h * HALF:(h + 1) * HALF] = low
-
-    def piece(which, b, first, last):
+                mat[which, b, h * HALF:(h + 1) * HALF] = high
+                mat[which, b, BLOCK + h * HALF:BLOCK + (h + 1) * HALF] = low
+
+    def piece(which, c, b, first, last):
         columns = slice((first - b) * BLOCK, (last - b) * BLOCK)
-        return product(
-            mat_hi[which, b, :, columns], mat_lo[which, b, :, columns], both[first * BLOCK:last * BLOCK]
+        value = jnp.dot(
+            mat[which, b, :, columns], both[c, first * BLOCK:last * BLOCK], preferred_element_type=jnp.float32
         )
-
-    def inner(which):
+        return value[:BLOCK] + value[BLOCK:]
+
+    def inner(which, c):
         return [
-            piece(which, b, max(b, REACH), min(b + WIN, REACH + GROUP)) for b in range(GROUP)
+            piece(which, c, b, max(b, REACH), min(b + WIN, REACH + GROUP)) for b in range(GROUP)
         ]
 
-    def outer(which, n, sums):
-        wait_halo(n)
-        for w in (*range(REACH), *range(REACH + GROUP, 2 * REACH + GROUP)):
-            put(w, win[n, w])
+    def outer(which, c, sums):
         result = []
         for b in range(GROUP):
             value = sums[b]
             if b < REACH:
-                value = value + piece(which, b, b, REACH)
+                value = value + piece(which, c, b, b, REACH)
             if b + WIN > REACH + GROUP:
-                value = value + piece(which, b, REACH + GROUP, b + WIN)
-            result.append(value)
-        return result
+                value = value + piece(which, c, b, REACH + GROUP, b + WIN)
+            result.append(value + pltpu.roll(value, LANES // 2, 1))
+        return [jnp.where(left, result[2 * i], result[2 * i + 1]) for i in range(GROUP // 2)]
 
     receive_matrix(0)
-    image = outer(0, 0, inner(0))
-    for b in range(GROUP):
-        moved = old[o, m, b] + image[b]
-        win[1, REACH + b] = moved
-        total[b] = moved
-    send_halo(1)
-    for b in range(GROUP):
-        put(REACH + b, win[1, REACH + b])
+    sums = [inner(0, c) for c in range(CHUNKS)]
+    wait_halo(0, 0)
+    for side in range(2):
+        for w in range(REACH):
+            put_block(side * (REACH + GROUP) + w, edge[side, w])
+    start = [cross(left, old[o, m, 2 * i], old[o, m, 2 * i + 1]) for i in range(GROUP // 2)]
+    for c in range(CHUNKS):
+        image = outer(0, c, sums[c])
+        for i in range(GROUP // 2):
+            moved = start[i][c] + image[i]
+            state[0, c, i] = moved
+            total[c, i] = moved
+        send_halo(1, c)
+    for c in range(CHUNKS):
+        for i in range(GROUP // 2):
+            put_pair(c, REACH + 2 * i, state[0, c, i])
     relay_matrix(1)
     for j in range(1, GROUP):
         for i in range(1, GROUP):
@@ -273,8 +310,8 @@
             old_hi[core * GROUP + g] = high
             old_lo[core * GROUP + g] = low
 
+    sums = [inner(1, c) for c in range(CHUNKS)]
     for n in range(1, ORDER + 1):
-        sums = inner(1)
         if n == ORDER - 1:
             for j in range(1, GROUP):
                 for i in range(1, GROUP):
@@ -284,28 +321,40 @@
         if n == ORDER:
             old_cross().wait_recv()
             turn(other)
-        image = outer(1, n, sums)
-        scale = jnp.where(left, jnp.float32(1.0 / n), jnp.float32(-1.0 / n))
-        terms = [swap(value) * scale for value in image]
-        if n < ORDER:
-            for b in range(GROUP):
-                win[n + 1, REACH + b] = terms[b]
-            send_halo(n + 1)
-        for b in range(GROUP):
-            value = total[b] + terms[b]
-            total[b] = value
-            put(REACH + b, terms[b] if n < ORDER else value)
+        scale = jnp.where(even, jnp.float32(1.0 / n), jnp.float32(-1.0 / n))
+        for c in range(CHUNKS):
+            wait_halo(n, c)
+            for side in range(2):
+                put_pair(c, side * (REACH + GROUP), halo[n - 1, c, side])
+            terms = [swap(even, value) * scale for value in outer(1, c, sums[c])]
+            if n < ORDER:
+                for i in range(GROUP // 2):
+                    state[n, c, i] = terms[i]
+                send_halo(n + 1, c)
+            for i in range(GROUP // 2):
+                total[c, i] = total[c, i] + terms[i]
+            if n < ORDER:
+                for i in range(GROUP // 2):
+                    put_pair(c, REACH + 2 * i, terms[i])
+                sums[c] = inner(1, c)
+
+    for i in range(GROUP // 2):
+        ends = cross(left, total[0, i], total[1, i])
+        for h in range(2):
+            blocks_new[2 * i + h] = ends[h]
+            high, low = split(ends[h])
+            new[span(2 * i + h), :LANES] = high
+            new[span(2 * i + h), LANES:] = low
 
     def back_copy(j):
-        return remote(total.at[peer(j)], back.at[m], back_s.at[j], back_r.at[j], (base + peer(j), o))
+        return remote(blocks_new.at[peer(j)], back.at[m], back_s.at[j], back_r.at[j], (base + peer(j), o))
 
     for j in range(1, GROUP):
         back_copy(j).start()
-    back[m] = total[m]
-
-    sign = jnp.where(left, jnp.float32(1.0), jnp.float32(-1.0))
-    new = both[REACH * BLOCK:(REACH + GROUP) * BLOCK]
-    per = HALF // share
+    back[m] = blocks_new[m]
+
+    sign = jnp.where(even, jnp.float32(1.0), jnp.float32(-1.0))
+    per = QUARTER // share
 
     def part_copy(j):
         to = (s + j) % spaces
@@ -313,15 +362,18 @@
 
     for i in range(2 * GROUP):
         g = (i + (q + quads // 2) * 2 * GROUP // quads) % (2 * GROUP)
-        value = product(old_hi[g], old_lo[g], new)
-        value = value[:HALF] + swap(value[HALF:]) * sign
-        for r in range(per):
-            to = g * per + r
-            part[to] = value[r * share:(r + 1) * share]
-
-            @pl.when(to != s)
-            def _():
-                part_copy((to - s + spaces) % spaces).start()
+        value = product(old_hi[g], old_lo[g], new[...])
+        for c in range(CHUNKS):
+            lead = 2 * c * QUARTER
+            found = value[lead:lead + QUARTER] + swap(even, value[lead + QUARTER:lead + 2 * QUARTER]) * sign
+            first = ((g // 2) * 4 + 2 * c + g % 2) * per
+            for r in range(per):
+                to = first + r
+                part[to] = found[r * share:(r + 1) * share]
+
+                @pl.when(to != s)
+                def _():
+                    part_copy((to - s + spaces) % spaces).start()
 
     got[s] = part[s]
 
@@ -329,10 +381,7 @@
         back_copy(j).wait_recv()
     for t in range(2):
         columns = slice(t * LANES, (t + 1) * LANES)
-        first = back[2 * t]
-        second = back[2 * t + 1]
-        prop[0, 0, :, columns] = jnp.where(left, first, swap(second))
-        prop[1, 0, :, columns] = jnp.where(left, swap(first), second)
+        prop[0, 0, :, columns], prop[1, 0, :, columns] = pair(even, back[2 * t], back[2 * t + 1])
 
     for j in range(1, GROUP):
         a2a(j).wait_send()
@@ -347,8 +396,10 @@
             for i in range(GROUP):
                 mat_cross(which, i, p).wait_send()
     old_cross().wait_send()
-    for n in range(ORDER + 1):
-        done_halo(n)
+    done_halo(0, 0)
+    for n in range(1, ORDER + 1):
+        for c in range(CHUNKS):
+            done_halo(n, c)
 
     @pl.loop(1, spaces)
     def _(j):
@@ -362,9 +413,7 @@
         sums.append(value * (1.0 / (spaces * BLOCK)))
     for t in range(2):
         columns = slice(t * LANES, (t + 1) * LANES)
-        first, second = sums[2 * t], sums[2 * t + 1]
-        proj[0, :, columns] = jnp.where(left, first, swap(second))
-        proj[1, :, columns] = jnp.where(left, swap(first), second)
+        proj[0, :, columns], proj[1, :, columns] = pair(even, sums[2 * t], sums[2 * t + 1])
 
     @pl.loop(1, spaces)
     def _(j):
@@ -395,12 +444,15 @@
                 pltpu.SMEM(pattern.shape, jnp.int32),
                 dma((5,)),
                 pltpu.VMEM((2, GROUP, GROUP, BLOCK, LANES), f32),
-                pltpu.VMEM((ORDER + 1, 2 * REACH + GROUP, BLOCK, LANES), f32),
+                pltpu.VMEM((2, REACH, BLOCK, LANES), f32),
+                pltpu.VMEM((ORDER, CHUNKS, 2, BLOCK, LANES), f32),
+                pltpu.VMEM((ORDER, CHUNKS, 2, BLOCK, LANES), f32),
                 pltpu.VMEM((2, GROUP, 2, 2, HALF // 2, WIN * BLOCK), f32),
-                pltpu.VMEM((2, GROUP, BLOCK, WIN * BLOCK), bf16),
-                pltpu.VMEM((2, GROUP, BLOCK, WIN * BLOCK), bf16),
-                pltpu.VMEM(((2 * REACH + GROUP) * BLOCK, 2 * LANES), bf16),
+                pltpu.VMEM((2, GROUP, 2 * BLOCK, WIN * BLOCK), bf16),
+                pltpu.VMEM((CHUNKS, (2 * REACH + GROUP) * BLOCK, LANES), bf16),
+                pltpu.VMEM((CHUNKS, 2, BLOCK, LANES), f32),
                 pltpu.VMEM((GROUP, BLOCK, LANES), f32),
+                pltpu.VMEM((GROUP * BLOCK, 2 * LANES), bf16),
                 pltpu.VMEM((2 * GROUP, LANES, GROUP * BLOCK), bf16),
                 pltpu.VMEM((2 * GROUP, LANES, GROUP * BLOCK), bf16),
                 pltpu.VMEM((spaces, share, LANES), f32),
@@ -412,12 +464,12 @@
                 dma((2, GROUP, 2)), dma((2, GROUP, 2)),
                 dma((GROUP, GROUP)), dma((GROUP, GROUP)),
                 dma, dma,
-                dma((ORDER + 1, 2)), dma((ORDER + 1, 2)),
+                dma((ORDER + 1, CHUNKS, 2)), dma((ORDER + 1, CHUNKS, 2)),
                 dma((GROUP,)), dma((GROUP,)),
                 dma((spaces,)), dma((spaces,)),
             ],
             compiler_params=pltpu.CompilerParams(
-                collective_id=0, has_side_effects=True, vmem_limit_bytes=40 * 1024 * 1024
+                collective_id=0, has_side_effects=True, vmem_limit_bytes=64 * 1024 * 1024
             ),
             cost_estimate=pl.CostEstimate(flops=1200000000, bytes_accessed=3000000, transcendentals=0),
         )(coefficients, margin, step_matrix, neighbours, pattern)

time: 55 us -> 55.5 us (level)
  Pallas kernels: 48 us -> 52.3 us
  local copies, waits for them, and re-layouts: 6.04 us -> 2.34 us
    pallas_call x1, Pallas kernels: 48 us -> 52.3 us  [local(): pl.pallas_call(functools.partial(kernel, spaces), out_shape=(jax.ShapeDty...]
    unnamed x12 -> x4, local copies, waits for them, and re-layouts: 6.04 us -> 2.34 us
where the time goes in v3:
time: 55.5 us; the launch traced here: 55.3 us
  Pallas kernels  52.3 us (94%)
  local copies, waits for them, and re-layouts  2.34 us (4%)
  between operations  0.65 us (1%)
    pallas_call x1, Pallas kernels, local(): pl.pallas_call(functools.partial(kernel, spaces), out_shape=(jax.ShapeDty...  52.3 us
    unnamed x4, local copies, waits for them, and re-layouts  2.34 us

profile of v3, /device:TPU:0, one launch (start us, length us, event | category | flops | bytes accessed | tf_op | source)
XLA Modules:
  0.0 55.3 jit_solution(11532552599018772608)
XLA Ops:
  0.6 52.3 %shard_map.68 = (f32[2,1,128,256]{3,2,1,0:T(8,128)}, f32[2,32,256]{2,1,0:T(8,128)}) custom-call(f32[2,1,128,256]{3,2,1,0:T(8,128)} %coef_in.1, f32[1,16,128,128]{3,2,1,0:T(8,128)} %margin_in.1, f32[1,16,128,128]{3,2,1,0:T(8,128)} %step_in.1, s32[1,16]{1,0:T(1,128)} %nbr_in.1, s32[1,16]{1,0:T(1,128)} %pat_in.1), custom_call_target="tpu_custom_call" | custom-call | flops 1200000000 | bytes 3000000 | tf_op jit(solution)/shard_map/pallas_call | solution.py:432
  53.0 0.0 copy-start
  53.0 1.7 %copy.9 = f32[2,1,128,256]{3,2,1,0:T(8,128)} copy(f32[2,1,128,256]{3,2,1,0:T(8,128)} %get-tuple-element.4) | data formatting | bytes 524288
  54.7 0.0 copy-done
  54.7 0.6 %copy.10 = f32[2,32,256]{2,1,0:T(8,128)} copy(f32[2,32,256]{2,1,0:T(8,128)S(1)} %copy-done) | data formatting | bytes 131072
Async XLA Ops:
  53.0 1.7 %copy-start = (f32[2,32,256]{2,1,0:T(8,128)S(1)}, f32[2,32,256]{2,1,0:T(8,128)}, u32[]{:S(2)}) copy-start(f32[2,32,256]{2,1,0:T(8,128)} %get-tuple-element.5) | copy-start | bytes 196612

commit v4 on v3

--- a/solution.py
+++ b/solution.py
@@ -55,7 +55,7 @@
 
 def kernel(
     spaces, coef_in, margin_in, step_in, nbr_in, pat_in, prop, proj,
-    coef, raw, nbr, pat, load_sem, old, edge, halo, state, rows, mat, both, total, blocks_new, new, old_hi, old_lo, part, got, back,
+    coef, raw, nbr, pat, load_sem, old, edge, halo, state, rows, mat, both, acc, total, blocks_new, new, old_hi, old_lo, part, got, back,
     a2a_s, a2a_r, mat_s, mat_r, dia_s, dia_r, fwd_s, fwd_r, old_s, old_r, oldx_s, oldx_r,
     halo_s, halo_r, back_s, back_r, part_s, part_r,
 ):
@@ -99,17 +99,23 @@
         old[o, 2 * t, m], old[o, 2 * t + 1, m] = pair(even, real, imag)
 
     def compact(which):
-        sums = [None] * WIN
+        scales = []
         for k in range(nbr.shape[1]):
-            block = raw[which, k]
             live = jnp.float32(1.0) if k == 0 else pat[0, k].astype(jnp.float32)
+            scales.append([(nbr[0, k] == s + (d - REACH)).astype(jnp.float32) * live for d in range(WIN)])
+        deep = HALF // 4
+
+        @pl.loop(0, 4)
+        def _(i):
+            sums = [None] * WIN
+            for k in range(nbr.shape[1]):
+                block = raw[which, k, pl.ds(pl.multiple_of(i * deep, deep), deep), :]
+                for d in range(WIN):
+                    value = scales[k][d] * block
+                    sums[d] = value if sums[d] is None else sums[d] + value
             for d in range(WIN):
-                here = (nbr[0, k] == s + (d - REACH)).astype(jnp.float32) * live
-                value = here * block
-                sums[d] = value if sums[d] is None else sums[d] + value
-        for d in range(WIN):
-            for p in range(2):
-                rows[which, m, o, p, :, d * BLOCK:(d + 1) * BLOCK] = sums[d][p * HALF // 2:(p + 1) * HALF // 2]
+                at = pl.ds(pl.multiple_of((i % 2) * deep, deep), deep)
+                rows[which, m, o, i // 2, at, d * BLOCK:(d + 1) * BLOCK] = sums[d]
 
     def clear(side):
         zero = jnp.zeros((BLOCK, LANES), jnp.float32)
@@ -161,7 +167,7 @@
 
     def halo_copy(n, c, up):
         side = 0 if up else 1
-        if n == 0:
+        if isinstance(n, int) and n == 0:
             src = old.at[o, m, REACH:GROUP] if up else old.at[o, m, 0:REACH]
             dst = edge.at[side]
         else:
@@ -252,7 +258,8 @@
         for i in range(GROUP):
             for p in range(2):
                 mat_cross(which, i, p).wait_recv()
-        for b in range(GROUP):
+        @pl.loop(0, GROUP)
+        def _(b):
             for h in range(2):
                 high, low = split(rows[which, b, h].reshape(HALF, WIN * BLOCK))
                 mat[which, b, h * HALF:(h + 1) * HALF] = high
@@ -266,14 +273,13 @@
         return value[:BLOCK] + value[BLOCK:]
 
     def inner(which, c):
-        return [
-            piece(which, c, b, max(b, REACH), min(b + WIN, REACH + GROUP)) for b in range(GROUP)
-        ]
-
-    def outer(which, c, sums):
+        for b in range(GROUP):
+            acc[c, b] = piece(which, c, b, max(b, REACH), min(b + WIN, REACH + GROUP))
+
+    def outer(which, c):
         result = []
         for b in range(GROUP):
-            value = sums[b]
+            value = acc[c, b]
             if b < REACH:
                 value = value + piece(which, c, b, b, REACH)
             if b + WIN > REACH + GROUP:
@@ -282,22 +288,30 @@
         return [jnp.where(left, result[2 * i], result[2 * i + 1]) for i in range(GROUP // 2)]
 
     receive_matrix(0)
-    sums = [inner(0, c) for c in range(CHUNKS)]
+    both_chunks = functools.partial(pl.loop, 0, CHUNKS)
+
+    @both_chunks()
+    def _(c):
+        inner(0, c)
+
     wait_halo(0, 0)
     for side in range(2):
         for w in range(REACH):
             put_block(side * (REACH + GROUP) + w, edge[side, w])
-    start = [cross(left, old[o, m, 2 * i], old[o, m, 2 * i + 1]) for i in range(GROUP // 2)]
-    for c in range(CHUNKS):
-        image = outer(0, c, sums[c])
+    for i in range(GROUP // 2):
+        state[0, 0, i], state[0, 1, i] = cross(left, old[o, m, 2 * i], old[o, m, 2 * i + 1])
+
+    @both_chunks()
+    def _(c):
+        image = outer(0, c)
         for i in range(GROUP // 2):
-            moved = start[i][c] + image[i]
+            moved = state[0, c, i] + image[i]
             state[0, c, i] = moved
             total[c, i] = moved
         send_halo(1, c)
-    for c in range(CHUNKS):
         for i in range(GROUP // 2):
-            put_pair(c, REACH + 2 * i, state[0, c, i])
+            put_pair(c, REACH + 2 * i, total[c, i])
+
     relay_matrix(1)
     for j in range(1, GROUP):
         for i in range(1, GROUP):
@@ -305,38 +319,52 @@
     receive_matrix(1)
 
     def turn(core):
-        for g in range(GROUP):
+        @pl.loop(0, GROUP)
+        def _(g):
             high, low = split(old[core, g].reshape(GROUP * BLOCK, LANES).T)
             old_hi[core * GROUP + g] = high
             old_lo[core * GROUP + g] = low
 
-    sums = [inner(1, c) for c in range(CHUNKS)]
-    for n in range(1, ORDER + 1):
-        if n == ORDER - 1:
+    @both_chunks()
+    def _(c):
+        inner(1, c)
+
+    @pl.loop(1, ORDER + 1)
+    def _(n):
+        @pl.when(n == ORDER - 1)
+        def _():
             for j in range(1, GROUP):
                 for i in range(1, GROUP):
                     old_copy(j, i).wait_recv()
             old_cross().start()
-            turn(o)
-        if n == ORDER:
+
+        @pl.when(n == ORDER)
+        def _():
             old_cross().wait_recv()
-            turn(other)
-        scale = jnp.where(even, jnp.float32(1.0 / n), jnp.float32(-1.0 / n))
-        for c in range(CHUNKS):
+
+        @pl.when(n >= ORDER - 1)
+        def _():
+            turn((o + n + ORDER - 1) % 2)
+
+        scale = jnp.where(even, jnp.float32(1.0), jnp.float32(-1.0)) / n.astype(jnp.float32)
+
+        @both_chunks()
+        def _(c):
             wait_halo(n, c)
             for side in range(2):
                 put_pair(c, side * (REACH + GROUP), halo[n - 1, c, side])
-            terms = [swap(even, value) * scale for value in outer(1, c, sums[c])]
-            if n < ORDER:
+            terms = [swap(even, value) * scale for value in outer(1, c)]
+            for i in range(GROUP // 2):
+                total[c, i] = total[c, i] + terms[i]
+
+            @pl.when(n < ORDER)
+            def _():
                 for i in range(GROUP // 2):
                     state[n, c, i] = terms[i]
                 send_halo(n + 1, c)
-            for i in range(GROUP // 2):
-                total[c, i] = total[c, i] + terms[i]
-            if n < ORDER:
                 for i in range(GROUP // 2):
                     put_pair(c, REACH + 2 * i, terms[i])
-                sums[c] = inner(1, c)
+                inner(1, c)
 
     for i in range(GROUP // 2):
         ends = cross(left, total[0, i], total[1, i])
@@ -360,7 +388,8 @@
         to = (s + j) % spaces
         return remote(part.at[to], got.at[s], part_s.at[j], part_r.at[j], (to, o))
 
-    for i in range(2 * GROUP):
+    @pl.loop(0, 2 * GROUP)
+    def _(i):
         g = (i + (q + quads // 2) * 2 * GROUP // quads) % (2 * GROUP)
         value = product(old_hi[g], old_lo[g], new[...])
         for c in range(CHUNKS):
@@ -450,6 +479,7 @@
                 pltpu.VMEM((2, GROUP, 2, 2, HALF // 2, WIN * BLOCK), f32),
                 pltpu.VMEM((2, GROUP, 2 * BLOCK, WIN * BLOCK), bf16),
                 pltpu.VMEM((CHUNKS, (2 * REACH + GROUP) * BLOCK, LANES), bf16),
+                pltpu.VMEM((CHUNKS, GROUP, BLOCK, LANES), f32),
                 pltpu.VMEM((CHUNKS, 2, BLOCK, LANES), f32),
                 pltpu.VMEM((GROUP, BLOCK, LANES), f32),
                 pltpu.VMEM((GROUP * BLOCK, 2 * LANES), bf16),

time: 55.5 us -> 56.6 us (1.020)
  Pallas kernels: 52.3 us -> 53.5 us
    pallas_call x1, Pallas kernels: 52.3 us -> 53.5 us  [local(): pl.pallas_call(functools.partial(kernel, spaces), out_shape=(jax.ShapeDty...]
where the time goes in v4:
time: 56.6 us; the launch traced here: 56.5 us
  Pallas kernels  53.5 us (95%)
  local copies, waits for them, and re-layouts  2.34 us (4%)
  between operations  0.65 us (1%)
    pallas_call x1, Pallas kernels, local(): pl.pallas_call(functools.partial(kernel, spaces), out_shape=(jax.ShapeDty...  53.5 us
    unnamed x4, local copies, waits for them, and re-layouts  2.34 us

profile of v4, /device:TPU:0, one launch (start us, length us, event | category | flops | bytes accessed | tf_op | source)
XLA Modules:
  0.0 56.5 jit_solution(6533021638339592220)
XLA Ops:
  0.6 53.5 %shard_map.68 = (f32[2,1,128,256]{3,2,1,0:T(8,128)}, f32[2,32,256]{2,1,0:T(8,128)}) custom-call(f32[2,1,128,256]{3,2,1,0:T(8,128)} %coef_in.1, f32[1,16,128,128]{3,2,1,0:T(8,128)} %margin_in.1, f32[1,16,128,128]{3,2,1,0:T(8,128)} %step_in.1, s32[1,16]{1,0:T(1,128)} %nbr_in.1, s32[1,16]{1,0:T(1,128)} %pat_in.1), custom_call_target="tpu_custom_call" | custom-call | flops 1200000000 | bytes 3000000 | tf_op jit(solution)/shard_map/pallas_call | solution.py:461
  54.1 0.0 copy-start
  54.1 1.7 %copy.9 = f32[2,1,128,256]{3,2,1,0:T(8,128)} copy(f32[2,1,128,256]{3,2,1,0:T(8,128)} %get-tuple-element.4) | data formatting | bytes 524288
  55.8 0.0 copy-done
  55.8 0.6 %copy.10 = f32[2,32,256]{2,1,0:T(8,128)} copy(f32[2,32,256]{2,1,0:T(8,128)S(1)} %copy-done) | data formatting | bytes 131072
Async XLA Ops:
  54.1 1.7 %copy-start = (f32[2,32,256]{2,1,0:T(8,128)S(1)}, f32[2,32,256]{2,1,0:T(8,128)}, u32[]{:S(2)}) copy-start(f32[2,32,256]{2,1,0:T(8,128)} %get-tuple-element.5) | copy-start | bytes 196612
